TPU v7x, 256 devices: a whole 4x4x8 slice. The times are simulated.
256 devices in a mesh: ctx: 64 (over x, z, y_hi), tp: 4 (over y_lo, core).
Axes of the slice: x: 4, y: 4 (y_hi: 2, y_lo: 2; y = y_hi * 2 + y_lo), z: 8, core: 2. Of those that a mesh axis runs over, the one named last changes fastest.
Arguments:
- queries: bfloat16 [65536, 2048], P('ctx', 'tp'), may hold values from -6 to 6
- keys: bfloat16 [65536, 2048], P('ctx', 'tp'), may hold values from -6 to 6
- values: bfloat16 [65536, 2048], P('ctx', 'tp'), may hold values from -6 to 6
- offsets: int32 [32, 2], replicated, may hold values from 0 to 15
- out_weight: bfloat16 [2048, 2048], P('tp'), may hold values from -0.125 to 0.125
Outputs:
- mixed: bfloat16 [65536, 2048], P(('ctx', 'tp'))
All inputs are finite; a program needn't handle non-finite values.
Results may differ from a plain program's by a relative error of at most 0.015.
Values may be sent and summed in bfloat16 or wider, within the bound.
No kernel may reach another device: no remote copies, remote signals or barrier semaphores. Data moves between devices by JAX's collectives and lax.ppermute only.
A program may use at most 128 MiB of HBM per device.

v0:
```python
import jax
import jax.numpy as jnp
from jax import lax
from jax.sharding import PartitionSpec as P

HEAD_DIM = 64
SECOND_DILATION = 8
SPAN_BITS = 3
THIRD_DILATION = 16


NEG = -1e30


def partner_2(shard, axis, stride):
    return lax.ppermute(shard, axis, [(i, i ^ 1 << stride) for i in range(lax.axis_size(axis))])


def select_rows(field, dilation, start_offset, heads_on_shard):
    count_of_rows = field.shape[0]
    shaped = field.reshape(count_of_rows // dilation, dilation, heads_on_shard, HEAD_DIM)
    picked = lax.broadcasted_iota(
        jnp.int32, (1, dilation, heads_on_shard, 1), 1
    ) == start_offset.reshape(1, 1, heads_on_shard, 1)
    return jnp.sum(jnp.where(picked, shaped, jnp.zeros_like(shaped)), axis=1)


def attend(inputs):
    query_per_head, key_per_head, value_per_head = inputs
    scores = jnp.dot(
        query_per_head, key_per_head.T, preferred_element_type=jnp.float32
    ) * HEAD_DIM ** (-0.5)
    peak = jnp.max(scores, axis=1)
    expo = jnp.exp(scores - peak[:, None])
    total = jnp.sum(expo, axis=1)
    summed = jnp.dot(expo.astype(jnp.bfloat16), value_per_head, preferred_element_type=jnp.float32)
    return (peak, total, summed)


def widen_pattern(peak, total, summed, dilation, start_offset, count_of_rows):
    heads_on_shard = peak.shape[0]
    hit = lax.broadcasted_iota(jnp.int32, (1, 1, dilation), 2) == start_offset.reshape(
        heads_on_shard, 1, 1
    )
    peak_full = jnp.where(hit, peak[:, :, None], NEG).reshape(heads_on_shard, count_of_rows)
    total_full = jnp.where(hit, total[:, :, None], 0.0).reshape(heads_on_shard, count_of_rows)
    summed_full = jnp.where(hit[:, :, :, None], summed[:, :, None, :], 0.0).reshape(
        heads_on_shard, count_of_rows, HEAD_DIM
    )
    return (peak_full, total_full, summed_full)


def local(queries, keys, values, offsets, out_weight):
    count_of_rows = queries.shape[0]
    heads_on_shard = queries.shape[1] // HEAD_DIM
    segment_width = heads_on_shard * HEAD_DIM
    shard_offsets = lax.dynamic_slice_in_dim(
        offsets, lax.axis_index("tp") * heads_on_shard, heads_on_shard, 0
    )
    nearby_offset = shard_offsets[:, 0] % SECOND_DILATION
    distant_offset = shard_offsets[:, 1] % THIRD_DILATION

    def heads_first(field):
        return field.reshape(field.shape[0], heads_on_shard, HEAD_DIM).transpose(1, 0, 2)

    local_parts = lax.map(attend, (heads_first(queries), heads_first(keys), heads_first(values)))
    nearby_query = select_rows(queries, SECOND_DILATION, nearby_offset, heads_on_shard)
    near_kv = jnp.stack(
        [
            select_rows(keys, SECOND_DILATION, nearby_offset, heads_on_shard).reshape(
                -1, segment_width
            ),
            select_rows(values, SECOND_DILATION, nearby_offset, heads_on_shard).reshape(
                -1, segment_width
            ),
        ]
    )
    for bit in range(SPAN_BITS):
        partner = partner_2(near_kv, "ctx", bit)
        near_kv = jnp.concatenate([near_kv, partner], axis=1)
    nearby_partials = lax.map(
        attend, (nearby_query.transpose(1, 0, 2), heads_first(near_kv[0]), heads_first(near_kv[1]))
    )
    nearby_partials = widen_pattern(
        nearby_partials[0],
        nearby_partials[1],
        nearby_partials[2],
        SECOND_DILATION,
        nearby_offset,
        count_of_rows,
    )
    distant_query = select_rows(queries, THIRD_DILATION, distant_offset, heads_on_shard).transpose(
        1, 0, 2
    )
    far_kv = jnp.stack(
        [
            select_rows(keys, THIRD_DILATION, distant_offset, heads_on_shard).reshape(
                -1, segment_width
            ),
            select_rows(values, THIRD_DILATION, distant_offset, heads_on_shard).reshape(
                -1, segment_width
            ),
        ]
    )
    far_rows = distant_query.shape[1]
    piece = lax.all_gather(far_kv, "ctx", axis=1, tiled=True)
    fold_peak = jnp.full((heads_on_shard, far_rows), NEG, jnp.float32)
    piece_k = heads_first(piece[0])
    piece_v = heads_first(piece[1])
    scores = jnp.einsum(
        "hld,hsd->hls", distant_query, piece_k, preferred_element_type=jnp.float32
    ) * HEAD_DIM ** (-0.5)
    new_peak = jnp.maximum(fold_peak, jnp.max(scores, axis=2))
    expo = jnp.exp(scores - new_peak[:, :, None])
    fold_total = jnp.sum(expo, axis=2)
    fold_summed = jnp.einsum(
        "hls,hsd->hld", expo.astype(jnp.bfloat16), piece_v, preferred_element_type=jnp.float32
    )
    distant_partials = (new_peak, fold_total, fold_summed)
    distant_partials = widen_pattern(
        distant_partials[0],
        distant_partials[1],
        distant_partials[2],
        THIRD_DILATION,
        distant_offset,
        count_of_rows,
    )
    parts = [local_parts, nearby_partials, distant_partials]
    top = jnp.maximum(jnp.maximum(parts[0][0], parts[1][0]), parts[2][0])
    numer = jnp.zeros((heads_on_shard, count_of_rows, HEAD_DIM), jnp.float32)
    denom = jnp.zeros((heads_on_shard, count_of_rows), jnp.float32)
    for peak, total, summed in parts:
        factor = jnp.exp(peak - top)
        numer = numer + factor[:, :, None] * summed
        denom = denom + factor * total
    attn = (
        (numer / denom[:, :, None])
        .astype(jnp.bfloat16)
        .transpose(1, 0, 2)
        .reshape(count_of_rows, segment_width)
    )
    mixed = lax.psum_scatter(
        jnp.dot(attn, out_weight, preferred_element_type=jnp.float32).astype(jnp.bfloat16),
        "tp",
        scatter_dimension=0,
        tiled=True,
    )
    return mixed


def solution(mesh):
    return jax.shard_map(
        local,
        mesh=mesh,
        in_specs=(P("ctx", "tp"), P("ctx", "tp"), P("ctx", "tp"), P(), P("tp", None)),
        out_specs=P(("ctx", "tp"), None),
        check_vma=False,
    )
```

profile of v0, /device:TPU:1, one launch (start us, length us, event | category | flops | bytes accessed | tf_op | source)
XLA Modules:
  0.0 332.6 jit_solution(5016633176902496921)
XLA Ops:
  7.5 4.0 %reshape.280 = bf16[64,16,8,64]{3,2,1,0:T(8,128)(2,1)} reshape(bf16[1024,512]{1,0:T(8,128)(2,1)} %param.9) | data formatting | bytes 2097152 | tf_op jit(solution)/shard_map/reshape | solution.py:21
  11.4 3.9 %reshape.281 = bf16[64,16,8,64]{3,2,1,0:T(8,128)(2,1)} reshape(bf16[1024,512]{1,0:T(8,128)(2,1)} %param.10) | data formatting | bytes 2097152 | tf_op jit(solution)/shard_map/reshape | solution.py:21
  15.3 2.1 reshape.282
  17.4 6.0 %select_reduce_fusion.2 = (bf16[64,8,64]{2,1,0:T(8,128)(2,1)}, bf16[64,8,64]{2,1,0:T(8,128)(2,1)S(1)}, bf16[64,8,64]{2,1,0:T(8,128)(2,1)S(1)}) fusion(bf16[64,16,8,64]{3,2,1,0:T(8,128)(2,1)} %reshape.280, pred[16,8]{1,0:T(8,128)(4,1)S(1)} %iota_compare_fusion, bf16[64,16,8,64]{3,2,1,0:T(8,128)(2,1)} %reshape.281, bf16[64,16,8,64]{3,2,1,0:T(8,128)(2,1)} %reshape.282), kind=kLoop, calls=%fused_computation.51 | loop fusion | flops 3047424 | bytes 3342464 | tf_op jit(solution)/shard_map/reduce_sum | solution.py:25
  24.7 2.1 reshape.277
  26.8 3.9 %reshape.278 = bf16[128,8,8,64]{3,2,1,0:T(8,128)(2,1)} reshape(bf16[1024,512]{1,0:T(8,128)(2,1)} %param.10) | data formatting | bytes 2097152 | tf_op jit(solution)/shard_map/reshape | solution.py:21
  30.7 3.9 %reshape.279 = bf16[128,8,8,64]{3,2,1,0:T(8,128)(2,1)} reshape(bf16[1024,512]{1,0:T(8,128)(2,1)} %param.11) | data formatting | bytes 2097152 | tf_op jit(solution)/shard_map/reshape | solution.py:21
  34.6 6.4 %select_reduce_fusion.4 = (bf16[128,8,64]{2,1,0:T(8,128)(2,1)S(1)}, bf16[128,8,64]{2,1,0:T(8,128)(2,1)}, bf16[128,8,64]{2,1,0:T(8,128)(2,1)}) fusion(bf16[128,8,8,64]{3,2,1,0:T(8,128)(2,1)} %reshape.278, pred[8,8]{1,0:T(8,128)(4,1)S(1)} %get-tuple-element.179, bf16[128,8,8,64]{3,2,1,0:T(8,128)(2,1)} %reshape.279, bf16[128,8,8,64]{3,2,1,0:T(8,128)(2,1)} %reshape.277), kind=kLoop, calls=%fused_computation.53 | loop fusion | flops 2949120 | bytes 3539008 | tf_op jit(solution)/shard_map/reduce_sum | solution.py:25
  42.4 3.8 %collective-permute-start = (bf16[2,128,512]{1,2,0:T(8,128)(2,1)S(1)}, bf16[2,128,512]{1,2,0:T(8,128)(2,1)S(1)}, u32[]{:S(2)}, u32[]{:S(2)}) collective-permute-start(bf16[2,128,512]{1,2,0:T(8,128)(2,1)S(1)} %pad_maximum_fusion.3), channel_id=1, source_target_pairs={{0,4},{4,0},{8,12},{12,8},{16,20},{20,16},{24,28},{28,24},{32,36},... | collective-permute-start | bytes 786440 | tf_op jit(solution)/shard_map/ppermute | solution.py:16
  46.2 5.0 %collective-permute-done = bf16[2,128,512]{1,2,0:T(8,128)(2,1)S(1)} collective-permute-done((bf16[2,128,512]{1,2,0:T(8,128)(2,1)S(1)}, bf16[2,128,512]{1,2,0:T(8,128)(2,1)S(1)}, u32[]{:S(2)}, u32[]{:S(2)}) %collective-permute-start) | collective-permute-done | bytes 262176 | tf_op jit(solution)/shard_map/ppermute | solution.py:16
  52.8 2.4 collective-permute-start.1
  58.0 2.3 copy.32
  60.4 7.5 %collective-permute-done.1 = bf16[2,256,512]{1,2,0:T(8,128)(2,1)} collective-permute-done((bf16[2,256,512]{1,2,0:T(8,128)(2,1)}, bf16[2,256,512]{1,2,0:T(8,128)(2,1)}, u32[]{:S(2)}, u32[]{:S(2)}) %collective-permute-start.1) | collective-permute-done | bytes 524320 | tf_op jit(solution)/shard_map/ppermute | solution.py:16
  67.8 2.2 pad_maximum_fusion.1
  70.0 3.2 collective-permute-start.2
  73.2 40.8 %while.30 = (s32[]{:T(128)}, f32[8,1024]{1,0:T(8,128)S(1)}, f32[8,1024]{1,0:T(8,128)S(1)}, f32[8,1024,64]{1,2,0:T(8,128)}, bf16[8,1024,64]{1,2,0:T(8,128)(2,1)},...) while((s32[]{:T(128)}, f32[8,1024]{1,0:T(8,128)S(1)}, f32[8,1024]{1,0:T(8,128)S(1)}, ...), condition=%wide.region_3.4_spmd.clone, body=%wide.region_0.3_spmd.sunk.clone | while | flops 276822016 | bytes 13273173 | solution.py:66
  73.2 1.7 multiply_reduce_fusion.4
  74.9 2.4 fusion.78
  78.3 1.7 multiply_reduce_fusion.4
  80.0 2.4 fusion.78
  83.4 1.7 multiply_reduce_fusion.4
  85.1 2.5 fusion.78
  88.5 1.7 multiply_reduce_fusion.4
  90.2 2.5 fusion.78
  93.6 1.7 multiply_reduce_fusion.4
  95.3 2.4 fusion.78
  98.7 1.7 multiply_reduce_fusion.4
  100.4 2.5 fusion.78
  103.9 1.7 multiply_reduce_fusion.4
  105.5 2.5 fusion.78
  109.0 1.7 multiply_reduce_fusion.4
  110.6 2.5 fusion.78
  114.1 1.7 copy.39
  116.5 3.8 %copy.46 = f32[8,1024,64]{2,1,0:T(8,128)} copy(f32[8,1024,64]{1,2,0:T(8,128)} %get-tuple-element.85) | data formatting | bytes 4194304 | tf_op jit(solution)/shard_map/while | solution.py:66
  120.3 5.2 %collective-permute-done.2 = bf16[2,512,512]{1,2,0:T(8,128)(2,1)} collective-permute-done((bf16[2,512,512]{1,2,0:T(8,128)(2,1)}, bf16[2,512,512]{1,2,0:T(8,128)(2,1)}, u32[]{:S(2)}, u32[]{:S(2)}) %collective-permute-start.2) | collective-permute-done | bytes 1048608 | tf_op jit(solution)/shard_map/ppermute | solution.py:16
  125.5 1.6 pad_maximum_fusion
  128.3 19.4 %while.31 = (s32[]{:T(128)}, f32[8,128]{1,0:T(8,128)S(1)}, f32[8,128]{1,0:T(8,128)S(1)}, f32[8,128,64]{1,2,0:T(8,128)}, bf16[8,128,64]{2,1,0:T(8,128)(2,1)}, /*i...) while((s32[]{:T(128)}, f32[8,128]{1,0:T(8,128)S(1)}, f32[8,128]{1,0:T(8,128)S(1)}, ...), condition=%wide.region_10.11_spmd.clone, body=%wide.region_7.10_spmd.sunk.clone | while | flops 34340608 | bytes 1906773 | solution.py:81
  149.8 45.6 %all-gather.2.cloned.1.call-done = bf16[2,4096,512]{2,0,1:T(2,128)(2,1)} async-done(((bf16[2,64,512]{2,0,1:T(2,128)(2,1)}), bf16[2,4096,512]{2,0,1:T(2,128)(2,1)}) %all-gather.2.cloned.1.call-update) | async-done | bytes 8388624 | tf_op jit(solution)/shard_map/all_gather | solution.py:106
  195.4 17.1 %fusion.51 = (bf16[1,4096,512]{2,0,1:T(2,128)(2,1)}, bf16[1,4096,512]{2,0,1:T(2,128)(2,1)}) fusion(bf16[2,4096,512]{2,0,1:T(2,128)(2,1)} %all-gather.2.cloned.1.call-done), kind=kLoop, calls=%fused_computation.82 | loop fusion | bytes 16777216 | tf_op jit(solution)/shard_map/slice | solution.py:109
  212.5 18.5 %copy.44 = bf16[1,4096,512]{1,2,0:T(8,128)(2,1)} copy(bf16[1,4096,512]{2,0,1:T(2,128)(2,1)} %get-tuple-element.174) | data formatting | bytes 8388608 | tf_op jit(solution)/shard_map/slice | solution.py:108
  231.0 3.5 %multiply_reduce_fusion.1 = (f32[8,64]{1,0:T(8,128)S(1)}, f32[8,64,4096]{2,1,0:T(8,128)S(1)}) fusion(bf16[8,4096,64]{1,2,0:T(8,128)(2,1)} %bitcast.134, bf16[8,64,64]{2,0,1:T(8,128)(2,1)S(1)} %bitcast.153), kind=kOutput, calls=%fused_computation.33 | convolution fusion | flops 272629248 | bytes 12650496 | tf_op jit(solution)/shard_map/hld,hsd->hls/dot_general | solution.py:110
  236.0 1.7 copy-done.1
  238.3 18.4 %copy.48 = bf16[1,4096,512]{1,2,0:T(8,128)(2,1)} copy(bf16[1,4096,512]{2,0,1:T(2,128)(2,1)} %get-tuple-element.173) | data formatting | bytes 8388608 | tf_op jit(solution)/shard_map/slice | solution.py:109
  256.7 6.3 %fusion.35 = f32[8,64,64]{2,1,0:T(8,128)S(1)} fusion(bf16[8,4096,64]{1,2,0:T(8,128)(2,1)} %bitcast.135, f32[8,64,4096]{2,1,0:T(8,128)} %copy-done.1, f32[8,64]{1,0:T(8,128)S(1)} %broadcast_maximum_fusion), kind=kOutput, calls=%fused_computation.36 | convolution fusion | flops 274726912 | bytes 12716032 | tf_op jit(solution)/shard_map/hls,hsd->hld/dot_general | solution.py:116
  263.1 8.9 %fusion.44 = bf16[8,1024,64]{2,1,0:T(8,128)(2,1)} fusion(f32[8,1024,64]{2,1,0:T(8,128)S(1)} %copy-done.2, f32[8,1024]{1,0:T(8,128)S(1)} %get-tuple-element.165, f32[8,64,64]{2,1,0:T(8,128)S(1)} %fusion.35, f32[8,1024]{1,0:T(8,128)S(1)} %get-tuple-element.168, f32[8,128,64]{2,1,0:T(8,128)S(1)} %copy.47, f32[8,1024]{1,0:T(8,128)S(1)} %get-tuple-element.167, ...), kind=kLoop, calls=%fused_computation.46 | loop fusion | flops 4718592 | bytes 3686400 | tf_op jit(solution)/shard_map/convert_element_type | solution.py:138
  272.0 1.9 copy.49
  273.9 4.3 %convolution_convert_fusion = bf16[1024,2048]{1,0:T(8,128)(2,1)} fusion(bf16[1024,512]{0,1:T(8,128)(2,1)S(1)} %bitcast.151, bf16[512,2048]{1,0:T(8,128)(2,1)S(1)} %copy-done), kind=kOutput, calls=%fused_computation.47 | convolution fusion | flops 2149580800 | bytes 7340032 | tf_op jit(solution)/shard_map/dot_general | solution.py:143
  278.3 47.5 %reduce-scatter.2.cloned.1.call-done = bf16[256,2048]{1,0:T(8,128)(2,1)} async-done(((bf16[1024,2048]{1,0:T(8,128)(2,1)}), bf16[256,2048]{1,0:T(8,128)(2,1)}) %reduce-scatter.2.cloned.1.call-update) | async-done | bytes 1048592 | tf_op jit(solution)/shard_map/reduce_scatter | solution.py:142
  (120 shorter events, 40.8 us)
Async XLA Ops:
  6.5 267.4 %copy-start = (bf16[512,2048]{1,0:T(8,128)(2,1)S(1)}, bf16[512,2048]{1,0:T(8,128)(2,1)}, u32[]{:S(2)}) copy-start(bf16[512,2048]{1,0:T(8,128)(2,1)} %param.13) | copy-start | bytes 6291460
  6.5 8.8 %copy-start.4 = (bf16[1024,512]{1,0:T(8,128)(2,1)S(1)}, bf16[1024,512]{1,0:T(8,128)(2,1)}, u32[]{:S(2)}) copy-start(bf16[1024,512]{1,0:T(8,128)(2,1)} %param.11) | copy-start | bytes 3145732
  6.5 188.8 %all-gather.2.cloned.1.call-start = ((), (), s32[]{:S(2)}) async-start(), calls=%async_computation.1 | async-start | bytes 8519680 | tf_op jit(solution)/shard_map/all_gather | solution.py:106
  17.4 7.3 %copy-start.3 = (bf16[1024,512]{1,0:T(8,128)(2,1)S(1)}, bf16[1024,512]{1,0:T(8,128)(2,1)}, u32[]{:S(2)}) copy-start(bf16[1024,512]{1,0:T(8,128)(2,1)} %param.9) | copy-start | bytes 3145732
  24.6 301.1 %reduce-scatter.2.cloned.1.call-start = ((), (), s32[]{:S(2)}) async-start(), calls=%async_computation.2 | async-start | bytes 5242880 | tf_op jit(solution)/shard_map/reduce_scatter | solution.py:142
  42.4 8.8 %collective-permute-start = (bf16[2,128,512]{1,2,0:T(8,128)(2,1)S(1)}, bf16[2,128,512]{1,2,0:T(8,128)(2,1)S(1)}, u32[]{:S(2)}, u32[]{:S(2)}) collective-permute-start(bf16[2,128,512]{1,2,0:T(8,128)(2,1)S(1)} %pad_maximum_fusion.3), channel_id=1, source_target_pairs={{0,4},{4,0},{8,12},{12,8},{16,20},{20,16},{24,28},{28,24},{32,36},... | collective-permute-start | bytes 786440 | tf_op jit(solution)/shard_map/ppermute | solution.py:16
  51.2 0.7 copy-start.5
  52.8 15.0 %collective-permute-start.1 = (bf16[2,256,512]{1,2,0:T(8,128)(2,1)}, bf16[2,256,512]{1,2,0:T(8,128)(2,1)}, u32[]{:S(2)}, u32[]{:S(2)}) collective-permute-start(bf16[2,256,512]{1,2,0:T(8,128)(2,1)} %pad_maximum_fusion.2), channel_id=1, source_target_pairs={{0,8},{4,12},{8,0},{12,4},{16,24},{20,28},{24,16},{28,20},{32,40},... | collective-permute-start | bytes 1572872 | tf_op jit(solution)/shard_map/ppermute | solution.py:16
  70.0 55.5 %collective-permute-start.2 = (bf16[2,512,512]{1,2,0:T(8,128)(2,1)}, bf16[2,512,512]{1,2,0:T(8,128)(2,1)}, u32[]{:S(2)}, u32[]{:S(2)}) collective-permute-start(bf16[2,512,512]{1,2,0:T(8,128)(2,1)} %pad_maximum_fusion.1), channel_id=1, source_target_pairs={{0,16},{4,20},{8,24},{12,28},{16,0},{20,4},{24,8},{28,12},{32,48},... | collective-permute-start | bytes 3145736 | tf_op jit(solution)/shard_map/ppermute | solution.py:16
  114.1 11.4 %copy-start.6 = (bf16[2,128,512]{1,2,0:T(8,128)(2,1)S(1)}, bf16[2,128,512]{1,2,0:T(8,128)(2,1)}, u32[]{:S(2)}) copy-start(bf16[2,128,512]{1,2,0:T(8,128)(2,1)} %copy-done.5) | copy-start | bytes 786436
  212.5 18.5 %copy-start.7 = (bf16[64,8,64]{2,1,0:T(8,128)(2,1)S(1)}, bf16[64,8,64]{2,1,0:T(8,128)(2,1)}, u32[]{:S(2)}) copy-start(bf16[64,8,64]{2,1,0:T(8,128)(2,1)} %get-tuple-element.131) | copy-start | bytes 196612
  234.5 3.2 copy-start.1
  256.7 6.3 %copy-start.2 = (f32[8,1024,64]{2,1,0:T(8,128)S(1)}, f32[8,1024,64]{2,1,0:T(8,128)}, u32[]{:S(2)}) copy-start(f32[8,1024,64]{2,1,0:T(8,128)} %copy.46) | copy-start | bytes 6291460
Sparse Core Ops, SparseCore 0:
  24.8 170.5 all-gather.1
  278.4 47.2 reduce-scatter.1
where the time goes:
time: 334 us; the launch traced here: 333 us
  waiting for transfers between devices  111 us (33%)
  local copies, waits for them, and re-layouts  97.9 us (29%)
  matrix products  64 us (19%)
  other arithmetic  36.3 us (11%)
  between operations  13.6 us (4%)
  starting transfers between devices  9.53 us (3%)
    reduce_scatter x1, waiting for transfers between devices, local(): lax.psum_scatter(jnp.dot(attn, out_weight, preferred_element_type=jnp.flo...  47.5 us
    all_gather x1, waiting for transfers between devices, local(): piece = lax.all_gather(far_kv, 'ctx', axis=1, tiled=True)  45.6 us
    slice x2, local copies, waits for them, and re-layouts, local(): piece_v = heads_first(piece[1])  35.5 us
    dot_general x16, matrix products, attend(): jnp.dot(expo.astype(jnp.bfloat16), value_per_head, preferred_element_type...  26.9 us
    dot_general x16, matrix products, attend(): jnp.dot(query_per_head, key_per_head.T, preferred_element_type=jnp.float32)  23.1 us
    reshape x6, local copies, waits for them, and re-layouts, select_rows(): field.reshape(count_of_rows // dilation, dilation, heads_on_shard, HEAD_DIM)  19.8 us
    slice x1, local copies, waits for them, and re-layouts, local(): piece_k = heads_first(piece[0])  18.5 us
    ppermute x3, waiting for transfers between devices, partner_2(): lax.ppermute(shard, axis, [(i, i ^ 1 << stride) for i in range(lax.axis_s...  17.6 us
  transfers between devices with their start and end apart: 5, of which 5 were waited for; matrix products, arithmetic and copies ran while one was open for 29% of the time, Pallas kernels for 0%

commit v1 on v0

v1 whole, which is shorter than its diff:
```python
import functools

import jax
import jax.numpy as jnp
from jax import lax
from jax.experimental import pallas as pl
from jax.experimental.pallas import tpu as pltpu
from jax.sharding import PartitionSpec as P

HEAD_DIM = 64
NEAR_DILATION = 8
FAR_DILATION = 16
SEGMENT = 8
ROWS = 1024
NEAR_ROWS = ROWS // NEAR_DILATION
FAR_ROWS = ROWS // FAR_DILATION
PICKED = NEAR_ROWS + FAR_ROWS
SENT_ROWS = PICKED + PICKED // 2
PAIR = 2 * HEAD_DIM
NEG = -1e30
SCALE = HEAD_DIM ** -0.5
BF16 = jnp.bfloat16
F32 = jnp.float32
ROW_BLOCK = 256


def lanes(shape):
    return lax.broadcasted_iota(jnp.int32, shape, 1)


def one_hot(offset_near, offset_far):
    row = lax.broadcasted_iota(jnp.int32, (PICKED, ROWS), 0)
    col = lax.broadcasted_iota(jnp.int32, (PICKED, ROWS), 1)
    at = jnp.where(
        row < NEAR_ROWS,
        row * NEAR_DILATION + offset_near,
        (row - NEAR_ROWS) * FAR_DILATION + offset_far,
    )
    return jnp.where(col == at, 1.0, 0.0).astype(BF16)


def pick_kernel(offsets_ref, q_ref, k_ref, v_ref, out_ref):
    pair = pl.program_id(0)
    for side in range(2):
        head = 2 * pair + side
        chosen = one_hot(offsets_ref[head, 0], offsets_ref[head, 1])
        q = jnp.dot(chosen, q_ref[...], preferred_element_type=F32)
        k = jnp.dot(chosen, k_ref[...], preferred_element_type=F32)
        v = jnp.dot(chosen, v_ref[...], preferred_element_type=F32)
        low = lanes((PICKED, PAIR)) < HEAD_DIM
        if side == 0:
            kv = jnp.where(low, k, pltpu.roll(v, HEAD_DIM, 1))
        else:
            kv = jnp.where(low, pltpu.roll(k, HEAD_DIM, 1), v)
        other = pltpu.roll(q, HEAD_DIM, 1)
        q_low, q_high = (q, other) if side == 0 else (other, q)
        q_packed = []
        for start, count in ((0, NEAR_ROWS), (NEAR_ROWS, FAR_ROWS)):
            half = count // 2
            q_packed.append(
                jnp.where(
                    lanes((half, PAIR)) < HEAD_DIM,
                    q_low[start : start + half],
                    q_high[start + half : start + count],
                )
            )
        out_ref[side, 0:PICKED, :] = kv.astype(BF16)
        out_ref[side, PICKED:SENT_ROWS, :] = (jnp.concatenate(q_packed, 0) * SCALE).astype(BF16)


def pick(queries, keys, values, offsets):
    heads = queries.shape[1] // HEAD_DIM
    pair_spec = pl.BlockSpec((ROWS, PAIR), lambda i: (0, i))
    return pl.pallas_call(
        pick_kernel,
        grid=(heads // 2,),
        in_specs=[pl.BlockSpec(memory_space=pltpu.SMEM)] + [pair_spec] * 3,
        out_specs=pl.BlockSpec((2, SENT_ROWS, PAIR), lambda i: (i, 0, 0)),
        out_shape=jax.ShapeDtypeStruct((heads, SENT_ROWS, PAIR), BF16),
        compiler_params=pltpu.CompilerParams(vmem_limit_bytes=32 * 1024 * 1024),
        cost_estimate=pl.CostEstimate(flops=10**9, bytes_accessed=4 * 10**6, transcendentals=0),
        name="pick_rows",
    )(offsets, queries, keys, values)


def contract_lanes(a, b):
    return lax.dot_general(a, b, (((1,), (1,)), ((), ())), preferred_element_type=F32)


def with_ones(v):
    return jnp.concatenate([v, jnp.ones_like(v)], 1)


def softmax_sum(scores, values):
    peak = functools.reduce(jnp.maximum, [jnp.max(s, axis=1, keepdims=True) for s in scores])
    acc = None
    for s, v in zip(scores, values):
        part = jnp.dot(jnp.exp(s - peak).astype(BF16), v, preferred_element_type=F32)
        acc = part if acc is None else acc + part
    total = acc[:, PAIR:]
    return acc[:, :PAIR] / total, peak + jnp.log(total)


def local_kernel(q_ref, k_ref, v_ref, out_ref, lse_ref):
    keys = k_ref[...]
    values = with_ones(v_ref[...])
    low = lanes((ROW_BLOCK, PAIR)) < HEAD_DIM
    zero = jnp.zeros((), BF16)

    def step(i, carry):
        rows = pl.ds(pl.multiple_of(i * ROW_BLOCK, ROW_BLOCK), ROW_BLOCK)
        q = q_ref[rows, :] * jnp.asarray(SCALE, BF16)
        both = [
            softmax_sum([contract_lanes(jnp.where(mine, q, zero), keys)], [values])
            for mine in (low, jnp.logical_not(low))
        ]
        out_ref[rows, :] = jnp.where(low, both[0][0], both[1][0]).astype(BF16)
        lse_ref[rows, :] = jnp.where(low, both[0][1], both[1][1])
        return carry

    lax.fori_loop(0, ROWS // ROW_BLOCK, step, 0)


def local_attention(queries, keys, values):
    pairs = queries.shape[1] // PAIR
    spec = pl.BlockSpec((ROWS, PAIR), lambda i: (0, i))
    return pl.pallas_call(
        local_kernel,
        grid=(pairs,),
        in_specs=[spec] * 3,
        out_specs=[spec] * 2,
        out_shape=[
            jax.ShapeDtypeStruct(queries.shape, BF16),
            jax.ShapeDtypeStruct(queries.shape, F32),
        ],
        compiler_params=pltpu.CompilerParams(vmem_limit_bytes=40 * 1024 * 1024),
        cost_estimate=pl.CostEstimate(
            flops=16 * 10**9, bytes_accessed=8 * 10**6, transcendentals=8 * 2**20
        ),
        name="local_attention",
    )(queries, keys, values)


def unpack_queries(packed):
    low = lanes(packed.shape) < HEAD_DIM
    wide = packed.astype(F32)
    top = jnp.where(low, wide, 0.0).astype(BF16)
    bottom = jnp.where(low, pltpu.roll(wide, HEAD_DIM, 1), 0.0).astype(BF16)
    return top, bottom


def result_rows(out, lse):
    high = lse.astype(BF16)
    rest = (lse - high.astype(F32)).astype(BF16)
    lane = lanes(out.shape)
    moved = pltpu.roll(out, HEAD_DIM, 1)
    stats = jnp.where(lane < HEAD_DIM + HEAD_DIM // 2, high.astype(F32), rest.astype(F32))
    return jnp.where(lane < HEAD_DIM, moved, stats).astype(BF16)


def spread_kernel(sent_ref, far0_ref, far1_ref, far2_ref, far3_ref, out_ref):
    near_kv = jnp.concatenate([sent_ref[i, 0:NEAR_ROWS, :] for i in range(SEGMENT)], 0)
    near_values = with_ones(near_kv)
    far = [r[...] for r in (far0_ref, far1_ref, far2_ref, far3_ref)]
    far_values = [with_ones(f) for f in far]

    def near_step(i, carry):
        packed = jnp.concatenate(
            [sent_ref[2 * i + j, PICKED : PICKED + NEAR_ROWS // 2, :] for j in range(2)], 0
        )
        half = NEAR_ROWS // 2
        top, bottom = unpack_queries(packed)
        q = jnp.concatenate([top, bottom], 0)
        out, lse = softmax_sum([contract_lanes(q, near_kv)], [near_values])
        res = result_rows(out, lse)
        for j in range(2):
            out_ref[2 * i + j, 0:half, :] = res[j * half : (j + 1) * half]
            out_ref[2 * i + j, half:NEAR_ROWS, :] = res[(2 + j) * half : (3 + j) * half]
        return carry

    lax.fori_loop(0, SEGMENT // 2, near_step, 0)

    def far_step(i, carry):
        half = FAR_ROWS // 2
        packed = jnp.concatenate(
            [sent_ref[4 * i + j, PICKED + NEAR_ROWS // 2 : SENT_ROWS, :] for j in range(4)], 0
        )
        top, bottom = unpack_queries(packed)
        q = jnp.concatenate([top, bottom], 0)
        out, lse = softmax_sum([contract_lanes(q, f) for f in far], far_values)
        res = result_rows(out, lse)
        for j in range(4):
            out_ref[4 * i + j, NEAR_ROWS : NEAR_ROWS + half, :] = res[j * half : (j + 1) * half]
            out_ref[4 * i + j, NEAR_ROWS + half : PICKED, :] = res[(4 + j) * half : (5 + j) * half]
        return carry

    lax.fori_loop(0, SEGMENT // 4, far_step, 0)


def spread_attention(sent, far):
    return pl.pallas_call(
        spread_kernel,
        in_specs=[pl.BlockSpec(memory_space=pltpu.VMEM)] * 5,
        out_specs=pl.BlockSpec(memory_space=pltpu.VMEM),
        out_shape=jax.ShapeDtypeStruct((SEGMENT, PICKED, PAIR), BF16),
        compiler_params=pltpu.CompilerParams(vmem_limit_bytes=40 * 1024 * 1024),
        cost_estimate=pl.CostEstimate(
            flops=6 * 10**9, bytes_accessed=2 * 10**6, transcendentals=3 * 2**20
        ),
        name="spread_attention",
    )(sent, *far)


def combine_kernel(offsets_ref, out_ref, lse_ref, back_ref, attn_ref):
    pair = pl.program_id(0)
    low_rows = lanes((ROWS, PAIR)) < HEAD_DIM
    position = lax.broadcasted_iota(jnp.int32, (ROWS, PAIR), 0)
    outs = [out_ref[...].astype(F32)]
    lses = [lse_ref[...]]
    for which, (start, count, dilation) in enumerate(
        ((0, NEAR_ROWS, NEAR_DILATION), (NEAR_ROWS, FAR_ROWS, FAR_DILATION))
    ):
        offset = [offsets_ref[2 * pair + side, which] for side in range(2)]
        row = lax.broadcasted_iota(jnp.int32, (ROWS, 2 * count), 0)
        col = lax.broadcasted_iota(jnp.int32, (ROWS, 2 * count), 1)
        at = jnp.where(
            col < count, col * dilation + offset[0], (col - count) * dilation + offset[1]
        )
        placed = jnp.where(row == at, 1.0, 0.0).astype(BF16)
        low = lanes((count, PAIR)) < HEAD_DIM
        first = back_ref[0, start : start + count, :].astype(F32)
        second = back_ref[1, start : start + count, :].astype(F32)
        high_first, rest_first = first[:, 64:65], first[:, 96:97]
        high_second, rest_second = second[:, 64:65], second[:, 96:97]
        zero = jnp.zeros((count, PAIR), F32)
        top = jnp.concatenate(
            [
                jnp.where(low, first, zero),
                jnp.where(low, high_first, zero),
                jnp.where(low, rest_first, zero),
            ],
            1,
        )
        bottom = jnp.concatenate(
            [
                jnp.where(low, zero, pltpu.roll(second, HEAD_DIM, 1)),
                jnp.where(low, zero, high_second),
                jnp.where(low, zero, rest_second),
            ],
            1,
        )
        wide = jnp.dot(
            placed, jnp.concatenate([top, bottom], 0).astype(BF16), preferred_element_type=F32
        )
        here = jnp.where(low_rows, offset[0], offset[1])
        hit = lax.rem(position, dilation) == here
        outs.append(wide[:, :PAIR])
        lses.append(jnp.where(hit, wide[:, PAIR : 2 * PAIR] + wide[:, 2 * PAIR :], NEG))
    top = jnp.maximum(jnp.maximum(lses[0], lses[1]), lses[2])
    numer, denom = 0.0, 0.0
    for out, lse in zip(outs, lses):
        weight = jnp.exp(lse - top)
        numer = numer + weight * out
        denom = denom + weight
    attn_ref[...] = (numer / denom).astype(BF16)


def combine(offsets, out, lse, back):
    pairs = out.shape[1] // PAIR
    spec = pl.BlockSpec((ROWS, PAIR), lambda i: (0, i))
    return pl.pallas_call(
        combine_kernel,
        grid=(pairs,),
        in_specs=[
            pl.BlockSpec(memory_space=pltpu.SMEM),
            spec,
            spec,
            pl.BlockSpec((2, PICKED, PAIR), lambda i: (i, 0, 0)),
        ],
        out_specs=spec,
        out_shape=jax.ShapeDtypeStruct(out.shape, BF16),
        compiler_params=pltpu.CompilerParams(vmem_limit_bytes=40 * 1024 * 1024),
        cost_estimate=pl.CostEstimate(flops=10**9, bytes_accessed=6 * 10**6, transcendentals=0),
        name="combine_patterns",
    )(offsets, out, lse, back)


def swap(shard, axis, bits):
    return lax.ppermute(shard, axis, [(i, i ^ bits) for i in range(lax.axis_size(axis))])


def local(queries, keys, values, offsets, out_weight):
    heads = queries.shape[1] // HEAD_DIM
    place = lax.axis_index("tp")
    upper, core = place // 2, place % 2
    mine = lax.dynamic_slice_in_dim(offsets, place * heads, heads, 0)
    mine = jnp.stack([mine[:, 0] % NEAR_DILATION, mine[:, 1] % FAR_DILATION], 1)

    picked = pick(queries, keys, values, mine)
    segments = [
        [s * SEGMENT + i for i in range(SEGMENT)]
        for s in range(lax.axis_size("ctx") // SEGMENT)
    ]
    sent = lax.all_to_all(picked, "ctx", 0, 0, axis_index_groups=segments, tiled=True)
    out, lse = local_attention(queries, keys, values)

    far_kv = sent[:, NEAR_ROWS:PICKED, :].reshape(SEGMENT * FAR_ROWS, PAIR)
    far_kv = jnp.concatenate([far_kv, swap(far_kv, "ctx", 8)], 0)
    far = [far_kv] + [swap(far_kv, "ctx", 16 * i) for i in (1, 2, 3)]

    back = spread_attention(sent, far)
    back = lax.all_to_all(back, "ctx", 0, 0, axis_index_groups=segments, tiled=True)
    attn = combine(mine, out, lse, back)

    half = ROWS // 2
    own = lax.dynamic_slice_in_dim(attn, upper * half, half, 0)
    away = lax.dynamic_slice_in_dim(attn, (1 - upper) * half, half, 0)
    came = swap(away, "tp", 2)
    n_tp = lax.axis_size("tp")
    n_ctx = lax.axis_size("ctx")
    other = [
        (c * n_tp + t, (c ^ 1) * n_tp + (t ^ 2)) for c in range(n_ctx) for t in range(n_tp)
    ]
    cut = out_weight.shape[0] // 2
    weight_there = jnp.concatenate(
        [
            swap(out_weight[:cut], "tp", 2),
            lax.ppermute(out_weight[cut:], ("ctx", "tp"), other),
        ],
        0,
    )
    share = jnp.dot(own, out_weight, preferred_element_type=F32) + jnp.dot(
        came, weight_there, preferred_element_type=F32
    )
    quarter = half // 2
    keep = lax.dynamic_slice_in_dim(share, core * quarter, quarter, 0)
    give = lax.dynamic_slice_in_dim(share, (1 - core) * quarter, quarter, 0).astype(BF16)
    return (keep + swap(give, "tp", 1).astype(F32)).astype(BF16)


def solution(mesh):
    return jax.shard_map(
        local,
        mesh=mesh,
        in_specs=(P("ctx", "tp"), P("ctx", "tp"), P("ctx", "tp"), P(), P("tp", None)),
        out_specs=P(("ctx", "tp"), None),
        check_vma=False,
    )
```

time: 334 us -> 128 us (0.38)
  waiting for transfers between devices: 111 us -> 20.3 us
  local copies, waits for them, and re-layouts: 97.9 us -> 12.9 us
  matrix products: 64 us -> 4.18 us
  Pallas kernels: 0 us -> 39.6 us
  other arithmetic: 36.3 us -> 2.92 us
  blocking collectives: 0 us -> 26.1 us
  between operations: 13.6 us -> 0.12 us
  starting transfers between devices: 9.53 us -> 20.7 us
    dot_general x35 -> x2, matrix products: 64 us -> 4.18 us  [the longest x1 2.83 us: local(): jnp.dot(came, weight_there, preferred_element_type=F32)]
    slice x4 -> x2, local copies, waits for them, and re-layouts: 55.2 us -> 1.6 us  [the longest x1 1.59 us: local(): out_weight[:cut]]
    reduce_scatter x1 -> x0, waiting for transfers between devices: 47.5 us -> none  [local(): lax.psum_scatter(jnp.dot(attn, out_weight, preferred_element_type=jnp.flo...]
    all_gather x1 -> x0, waiting for transfers between devices: 45.6 us -> none  [local(): piece = lax.all_gather(far_kv, 'ctx', axis=1, tiled=True)]
    pallas_call x0 -> x4, Pallas kernels: none -> 39.6 us  [the longest x1 19.2 us: local_attention(): pl.pallas_call(local_kernel, grid=(pairs,), in_specs=[spec] * 3, out_spec...]
    all_to_all x0 -> x1, blocking collectives: none -> 26.1 us  [local(): lax.all_to_all(picked, 'ctx', 0, 0, axis_index_groups=segments, tiled=True)]
    reduce_sum x19 -> x0, other arithmetic: 21.5 us -> none  [the longest x2 12.4 us: select_rows(): return jnp.sum(jnp.where(picked, shaped, jnp.zeros_like(shaped)), axis=1)]
    reshape x6 -> x0, local copies, waits for them, and re-layouts: 19.8 us -> none  [select_rows(): field.reshape(count_of_rows // dilation, dilation, heads_on_shard, HEAD_DIM)]
  transfers between devices with their start and end apart: 5 -> 9, of which waited for: 5 -> 6; matrix products, arithmetic and copies ran while one was open for 29% -> 1% of each run, Pallas kernels for 0% -> 28%
where the time goes in v1:
time: 128 us; the launch traced here: 127 us
  Pallas kernels  39.6 us (31%)
  blocking collectives  26.1 us (20%)
  starting transfers between devices  20.7 us (16%)
  waiting for transfers between devices  20.3 us (16%)
  local copies, waits for them, and re-layouts  12.9 us (10%)
  matrix products  4.18 us (3%)
  other arithmetic  2.92 us (2%)
    all_to_all x1, blocking collectives, local(): lax.all_to_all(picked, 'ctx', 0, 0, axis_index_groups=segments, tiled=True)  26.1 us
    ppermute x7, waiting for transfers between devices, swap(): lax.ppermute(shard, axis, [(i, i ^ bits) for i in range(lax.axis_size(axi...  20.3 us
    pallas_call x1, Pallas kernels, local_attention(): pl.pallas_call(local_kernel, grid=(pairs,), in_specs=[spec] * 3, out_spec...  19.2 us
    ppermute x7, starting transfers between devices, swap(): lax.ppermute(shard, axis, [(i, i ^ bits) for i in range(lax.axis_size(axi...  12.6 us
    unnamed x24, local copies, waits for them, and re-layouts  10.9 us
    pallas_call x1, Pallas kernels, spread_attention(): pl.pallas_call(spread_kernel, in_specs=[pl.BlockSpec(memory_space=pltpu.V...  10.6 us
    all_to_all x1, starting transfers between devices, local(): lax.all_to_all(back, 'ctx', 0, 0, axis_index_groups=segments, tiled=True)  7.39 us
    pallas_call x1, Pallas kernels, combine(): pl.pallas_call(combine_kernel, grid=(pairs,), in_specs=[pl.BlockSpec(memo...  5.61 us
  transfers between devices with their start and end apart: 9, of which 6 were waited for; matrix products, arithmetic and copies ran while one was open for 1% of the time, Pallas kernels for 28%

profile of v1, /device:TPU:1, one launch (start us, length us, event | category | flops | bytes accessed | tf_op | source)
XLA Modules:
  0.0 126.8 jit_solution(13135628413800717759)
XLA Ops:
  0.0 0.0 copy-start
  0.0 0.7 copy-done
  0.7 0.1 constant_dynamic-slice_fusion.1
  0.8 0.1 copy.8.offsets_ref
  0.9 0.0 copy-start.1
  0.9 1.2 copy-done.1
  2.1 0.0 copy-start.3
  2.1 1.2 copy-done.3
  3.3 1.2 copy-done.5
  4.5 4.3 %pick_rows.1 = bf16[8,288,128]{2,1,0:T(8,128)(2,1)S(1)} custom-call(s32[8,2]{1,0:T(8,128)S(1)} %copy.8.offsets_ref, bf16[1024,512]{1,0:T(8,128)(2,1)S(1)} %copy-done.1, bf16[1024,512]{1,0:T(8,128)(2,1)S(1)} %copy-done.3, bf16[1024,512]{1,0:T(8,128)(2,1)S(1)} %copy-done.5), custom_call_target="tpu_custom_call" | custom-call | flops 1000000000 | bytes 4000000 | tf_op jit(solution)/shard_map/pick_rows/pallas_call | solution.py:74
  8.8 26.1 %all_to_all.10.sent_ref = bf16[8,288,128]{2,1,0:T(8,128)(2,1)S(1)} all-to-all(bf16[8,288,128]{2,1,0:T(8,128)(2,1)S(1)} %pick_rows.1), channel_id=1, replica_groups={{0,4,8,12,16,20,24,28},{32,36,40,44,48,52,56,60},{64,68,72,76,80,84,88,..., dimensions={0} | all-to-all | bytes 1179648 | tf_op jit(solution)/shard_map/all_to_all | solution.py:304
  34.9 4.3 %collective-permute-start = (bf16[512,128]{1,0:T(8,128)(2,1)S(1)}, bf16[512,128]{1,0:T(8,128)(2,1)S(1)}, u32[]{:S(2)}, u32[]{:S(2)}) collective-permute-start(bf16[512,128]{1,0:T(8,128)(2,1)S(1)} %bitcast.3), channel_id=1, source_target_pairs={{0,32},{4,36},{8,40},{12,44},{16,48},{20,52},{24,56},{28,60},{32,0... | collective-permute-start | bytes 393224 | tf_op jit(solution)/shard_map/ppermute | solution.py:289
  39.2 3.6 %collective-permute-done = bf16[512,128]{1,0:T(8,128)(2,1)S(1)} collective-permute-done((bf16[512,128]{1,0:T(8,128)(2,1)S(1)}, bf16[512,128]{1,0:T(8,128)(2,1)S(1)}, u32[]{:S(2)}, u32[]{:S(2)}) %collective-permute-start) | collective-permute-done | bytes 131104 | tf_op jit(solution)/shard_map/ppermute | solution.py:289
  42.9 2.6 %collective-permute-start.3 = (bf16[1024,128]{1,0:T(8,128)(2,1)S(1)}, bf16[1024,128]{1,0:T(8,128)(2,1)S(1)}, u32[]{:S(2)}, u32[]{:S(2)}) collective-permute-start(bf16[1024,128]{1,0:T(8,128)(2,1)S(1)} %pad_maximum_fusion.far0_ref), channel_id=1, source_target_pairs={{0,192},{4,196},{8,200},{12,204},{16,208},{20,212},{24,216},{28,22... | collective-permute-start | bytes 786440 | tf_op jit(solution)/shard_map/ppermute | solution.py:289
  45.4 0.5 collective-permute-start.2
  45.9 0.3 collective-permute-start.1
  46.2 0.0 copy-done.10
  46.2 1.6 %fusion.9 = (bf16[256,2048]{1,0:T(8,128)(2,1)}, bf16[256,2048]{1,0:T(8,128)(2,1)}) fusion(bf16[512,2048]{1,0:T(8,128)(2,1)S(1)} %copy-done.10), kind=kLoop, calls=%fused_computation.22 | loop fusion | bytes 4194304 | tf_op jit(solution)/shard_map/slice | solution.py:327
  47.8 0.4 collective-permute-start.5
  48.2 0.7 collective-permute-start.6
  48.9 2.9 %collective-permute-done.3.far3_ref = bf16[1024,128]{1,0:T(8,128)(2,1)S(1)} collective-permute-done((bf16[1024,128]{1,0:T(8,128)(2,1)S(1)}, bf16[1024,128]{1,0:T(8,128)(2,1)S(1)}, u32[]{:S(2)}, u32[]{:S(2)}) %collective-permute-start.3) | collective-permute-done | bytes 262176 | tf_op jit(solution)/shard_map/ppermute | solution.py:289
  51.8 0.4 collective-permute-done.2.far2_ref
  52.2 0.9 collective-permute-done.1.far1_ref
  53.2 10.6 %spread_attention.1 = bf16[8,192,128]{2,1,0:T(8,128)(2,1)} custom-call(bf16[8,288,128]{2,1,0:T(8,128)(2,1)S(1)} %all_to_all.10.sent_ref, bf16[1024,128]{1,0:T(8,128)(2,1)S(1)} %pad_maximum_fusion.far0_ref, bf16[1024,128]{1,0:T(8,128)(2,1)S(1)} %collective-permute-done.1.far1_ref, bf16[1024,128]{1,0:T(8,128)(2,1)S(1)} %collective-permute-done.2.far2_ref, ...), custom_call_target="tpu_custom_call" | custom-call | flops 6000000000 | bytes 2000000 | tf_op jit(solution)/shard_map/spread_attention/pallas_call | solution.py:201
  63.8 7.4 %all-to-all-start.1 = ((bf16[8,192,128]{2,1,0:T(8,128)(2,1)}), bf16[8,192,128]{2,1,0:T(8,128)(2,1)S(1)}, u32[]{:S(2)}, u32[]{:S(2)}) async-start(bf16[8,192,128]{2,1,0:T(8,128)(2,1)} %spread_attention.1), calls=%async_computation.1 | async-start | bytes 786432 | tf_op jit(solution)/shard_map/all_to_all | solution.py:312
  71.2 0.0 copy-done.2
  71.2 0.0 copy-start.4
  71.2 1.2 copy-done.4
  72.4 1.2 copy-done.6
  73.6 19.2 %local_attention.1 = (bf16[1024,512]{1,0:T(8,128)(2,1)S(1)}, f32[1024,512]{1,0:T(8,128)S(1)}) custom-call(bf16[1024,512]{1,0:T(8,128)(2,1)S(1)} %copy-done.2, bf16[1024,512]{1,0:T(8,128)(2,1)S(1)} %copy-done.4, bf16[1024,512]{1,0:T(8,128)(2,1)S(1)} %copy-done.6), custom_call_target="tpu_custom_call" | custom-call | flops 16000000000 | bytes 8000000 | tf_op jit(solution)/shard_map/local_attention/pallas_call | solution.py:127
  92.8 0.0 copy-start.7
  92.8 1.0 copy-done.7
  93.8 0.0 all-to-all-done.1.back_ref
  93.8 1.2 copy-done.8
  95.0 5.6 %combine_patterns.1 = bf16[1024,512]{1,0:T(8,128)(2,1)S(1)} custom-call(s32[8,2]{1,0:T(8,128)S(1)} %copy.8.offsets_ref, bf16[1024,512]{1,0:T(8,128)(2,1)S(1)} %copy-done.8, f32[1024,512]{1,0:T(8,128)S(1)} %get-tuple-element.8.lse_ref, bf16[8,192,128]{2,1,0:T(8,128)(2,1)S(1)} %all-to-all-done.1.back_ref), custom_call_target="tpu_custom_call" | custom-call | flops 1000000000 | bytes 6000000 | tf_op jit(solution)/shard_map/combine_patterns/pallas_call | solution.py:271
  100.7 0.7 collective-permute-start.4
  101.3 0.0 collective-permute-done.5
  101.3 0.0 collective-permute-done.6
  101.3 10.1 %collective-permute-done.4 = bf16[512,512]{1,0:T(8,128)(2,1)S(1)} collective-permute-done((bf16[512,512]{1,0:T(8,128)(2,1)S(1)}, bf16[512,512]{1,0:T(8,128)(2,1)S(1)}, u32[]{:S(2)}, u32[]{:S(2)}) %collective-permute-start.4) | collective-permute-done | bytes 524320 | tf_op jit(solution)/shard_map/ppermute | solution.py:289
  111.5 2.8 %fusion = f32[512,2048]{1,0:T(8,128)S(1)} fusion(bf16[512,512]{1,0:T(8,128)(2,1)S(1)} %collective-permute-done.4, bf16[256,2048]{1,0:T(8,128)(2,1)} %collective-permute-done.6, bf16[256,2048]{1,0:T(8,128)(2,1)} %collective-permute-done.5), kind=kOutput, calls=%fused_computation.1 | convolution fusion | flops 1077936128 | bytes 6815744 | tf_op jit(solution)/shard_map/dot_general | solution.py:332
  114.3 0.0 copy-done.11
  114.3 1.3 %convolution_add_fusion = f32[512,2048]{1,0:T(8,128)S(1)} fusion(f32[512,2048]{1,0:T(8,128)S(1)} %fusion, bf16[512,2048]{1,0:T(8,128)(2,1)S(1)} %copy-done.11, bf16[1024,512]{1,0:T(8,128)(2,1)S(1)} %combine_patterns.1, s32[]{:T(128)S(6)} %select_n.42), kind=kOutput, calls=%fused_computation | convolution fusion | flops 1074790400 | bytes 11010052 | tf_op jit(solution)/shard_map/dot_general | solution.py:332
  115.7 0.0 copy-start.9
  115.7 1.9 %copy-done.9 = f32[512,2048]{1,0:T(8,128)} copy-done((f32[512,2048]{1,0:T(8,128)}, f32[512,2048]{1,0:T(8,128)S(1)}, u32[]{:S(2)}) %copy-start.9) | copy-done | bytes 4194328
  117.6 0.1 dynamic-slice_convert_fusion
  117.7 3.9 %collective-permute-start.7 = (bf16[256,2048]{1,0:T(8,128)(2,1)S(1)}, bf16[256,2048]{1,0:T(8,128)(2,1)S(1)}, u32[]{:S(2)}, u32[]{:S(2)}) collective-permute-start(bf16[256,2048]{1,0:T(8,128)(2,1)S(1)} %dynamic-slice_convert_fusion), channel_id=1, source_target_pairs={{0,1},{1,0},{2,3},{3,2},{4,5},{5,4},{6,7},{7,6},{8,9},{9,8},{10,11... | collective-permute-start | bytes 3145736 | tf_op jit(solution)/shard_map/ppermute | solution.py:289
  121.6 2.3 %collective-permute-done.7 = bf16[256,2048]{1,0:T(8,128)(2,1)S(1)} collective-permute-done((bf16[256,2048]{1,0:T(8,128)(2,1)S(1)}, bf16[256,2048]{1,0:T(8,128)(2,1)S(1)}, u32[]{:S(2)}, u32[]{:S(2)}) %collective-permute-start.7) | collective-permute-done | bytes 1048608 | tf_op jit(solution)/shard_map/ppermute | solution.py:289
  123.9 2.9 %add_convert_fusion = bf16[256,2048]{1,0:T(8,128)(2,1)} fusion(bf16[256,2048]{1,0:T(8,128)(2,1)S(1)} %collective-permute-done.7, f32[512,2048]{1,0:T(8,128)} %copy-done.9, s32[]{:T(128)S(6)} %select_n.45), kind=kLoop, calls=%fused_computation.5 | loop fusion | flops 1572864 | bytes 4194308 | tf_op jit(solution)/shard_map/convert_element_type | solution.py:338
  (11 shorter events, 0.1 us)
Async XLA Ops:
  0.0 0.7 copy-start
  0.9 1.2 copy-start.1
  2.1 1.2 copy-start.3
  3.3 1.2 copy-start.5
  4.5 41.7 %copy-start.10 = (bf16[512,2048]{1,0:T(8,128)(2,1)S(1)}, bf16[512,2048]{1,0:T(8,128)(2,1)}, u32[]{:S(2)}) copy-start(bf16[512,2048]{1,0:T(8,128)(2,1)} %param.9) | copy-start | bytes 6291460
  34.9 7.9 %collective-permute-start = (bf16[512,128]{1,0:T(8,128)(2,1)S(1)}, bf16[512,128]{1,0:T(8,128)(2,1)S(1)}, u32[]{:S(2)}, u32[]{:S(2)}) collective-permute-start(bf16[512,128]{1,0:T(8,128)(2,1)S(1)} %bitcast.3), channel_id=1, source_target_pairs={{0,32},{4,36},{8,40},{12,44},{16,48},{20,52},{24,56},{28,60},{32,0... | collective-permute-start | bytes 393224 | tf_op jit(solution)/shard_map/ppermute | solution.py:289
  42.9 9.0 %collective-permute-start.3 = (bf16[1024,128]{1,0:T(8,128)(2,1)S(1)}, bf16[1024,128]{1,0:T(8,128)(2,1)S(1)}, u32[]{:S(2)}, u32[]{:S(2)}) collective-permute-start(bf16[1024,128]{1,0:T(8,128)(2,1)S(1)} %pad_maximum_fusion.far0_ref), channel_id=1, source_target_pairs={{0,192},{4,196},{8,200},{12,204},{16,208},{20,212},{24,216},{28,22... | collective-permute-start | bytes 786440 | tf_op jit(solution)/shard_map/ppermute | solution.py:289
  45.4 6.8 %collective-permute-start.2 = (bf16[1024,128]{1,0:T(8,128)(2,1)S(1)}, bf16[1024,128]{1,0:T(8,128)(2,1)S(1)}, u32[]{:S(2)}, u32[]{:S(2)}) collective-permute-start(bf16[1024,128]{1,0:T(8,128)(2,1)S(1)} %pad_maximum_fusion.far0_ref), channel_id=1, source_target_pairs={{0,128},{4,132},{8,136},{12,140},{16,144},{20,148},{24,152},{28,15... | collective-permute-start | bytes 786440 | tf_op jit(solution)/shard_map/ppermute | solution.py:289
  45.9 7.2 %collective-permute-start.1 = (bf16[1024,128]{1,0:T(8,128)(2,1)S(1)}, bf16[1024,128]{1,0:T(8,128)(2,1)S(1)}, u32[]{:S(2)}, u32[]{:S(2)}) collective-permute-start(bf16[1024,128]{1,0:T(8,128)(2,1)S(1)} %pad_maximum_fusion.far0_ref), channel_id=1, source_target_pairs={{0,64},{4,68},{8,72},{12,76},{16,80},{20,84},{24,88},{28,92},{32,9... | collective-permute-start | bytes 786440 | tf_op jit(solution)/shard_map/ppermute | solution.py:289
  47.8 53.5 %collective-permute-start.5 = (bf16[256,2048]{1,0:T(8,128)(2,1)}, bf16[256,2048]{1,0:T(8,128)(2,1)}, u32[]{:S(2)}, u32[]{:S(2)}) collective-permute-start(bf16[256,2048]{1,0:T(8,128)(2,1)} %get-tuple-element.9), channel_id=1, source_target_pairs={{0,2},{1,3},{2,0},{3,1},{4,6},{5,7},{6,4},{7,5},{8,10},{9,11},{10,... | collective-permute-start | bytes 3145736 | tf_op jit(solution)/shard_map/ppermute | solution.py:289
  48.2 23.0 %copy-start.2 = (bf16[1024,512]{1,0:T(8,128)(2,1)S(1)}, bf16[1024,512]{1,0:T(8,128)(2,1)}, u32[]{:S(2)}) copy-start(bf16[1024,512]{1,0:T(8,128)(2,1)} %q_ref.3) | copy-start | bytes 3145732
  48.2 53.1 %collective-permute-start.6 = (bf16[256,2048]{1,0:T(8,128)(2,1)}, bf16[256,2048]{1,0:T(8,128)(2,1)}, u32[]{:S(2)}, u32[]{:S(2)}) collective-permute-start(bf16[256,2048]{1,0:T(8,128)(2,1)} %get-tuple-element.10), channel_id=1, source_target_pairs={{0,6},{1,7},{2,4},{3,5},{4,2},{5,3},{6,0},{7,1},{8,14},{9,15},{10,... | collective-permute-start | bytes 3145736 | tf_op jit(solution)/shard_map/ppermute | solution.py:328
  63.8 30.0 %all-to-all-start.1 = ((bf16[8,192,128]{2,1,0:T(8,128)(2,1)}), bf16[8,192,128]{2,1,0:T(8,128)(2,1)S(1)}, u32[]{:S(2)}, u32[]{:S(2)}) async-start(bf16[8,192,128]{2,1,0:T(8,128)(2,1)} %spread_attention.1), calls=%async_computation.1 | async-start | bytes 786432 | tf_op jit(solution)/shard_map/all_to_all | solution.py:312
  71.2 1.2 copy-start.4
  72.4 1.2 copy-start.6
  92.8 1.0 copy-start.7
  93.8 1.2 copy-start.8
  100.7 10.8 %collective-permute-start.4 = (bf16[512,512]{1,0:T(8,128)(2,1)S(1)}, bf16[512,512]{1,0:T(8,128)(2,1)S(1)}, u32[]{:S(2)}, u32[]{:S(2)}) collective-permute-start(bf16[512,512]{1,0:T(8,128)(2,1)S(1)} %constant_dynamic-slice_fusion), channel_id=1, source_target_pairs={{0,2},{1,3},{2,0},{3,1},{4,6},{5,7},{6,4},{7,5},{8,10},{9,11},{10,... | collective-permute-start | bytes 1572872 | tf_op jit(solution)/shard_map/ppermute | solution.py:289
  101.3 13.0 %copy-start.11 = (bf16[512,2048]{1,0:T(8,128)(2,1)S(1)}, bf16[512,2048]{1,0:T(8,128)(2,1)}, u32[]{:S(2)}) copy-start(bf16[512,2048]{1,0:T(8,128)(2,1)} %param.9) | copy-start | bytes 6291460
  115.7 1.9 %copy-start.9 = (f32[512,2048]{1,0:T(8,128)}, f32[512,2048]{1,0:T(8,128)S(1)}, u32[]{:S(2)}) copy-start(f32[512,2048]{1,0:T(8,128)S(1)} %convolution_add_fusion) | copy-start | bytes 12582916
  117.7 6.2 %collective-permute-start.7 = (bf16[256,2048]{1,0:T(8,128)(2,1)S(1)}, bf16[256,2048]{1,0:T(8,128)(2,1)S(1)}, u32[]{:S(2)}, u32[]{:S(2)}) collective-permute-start(bf16[256,2048]{1,0:T(8,128)(2,1)S(1)} %dynamic-slice_convert_fusion), channel_id=1, source_target_pairs={{0,1},{1,0},{2,3},{3,2},{4,5},{5,4},{6,7},{7,6},{8,9},{9,8},{10,11... | collective-permute-start | bytes 3145736 | tf_op jit(solution)/shard_map/ppermute | solution.py:289

commit v2 on v1

v2 whole, which is shorter than its diff:
```python
import functools

import jax
import jax.numpy as jnp
from jax import lax
from jax.experimental import pallas as pl
from jax.experimental.pallas import tpu as pltpu
from jax.sharding import PartitionSpec as P

HEAD_DIM = 64
NEAR_DILATION = 8
FAR_DILATION = 16
SEGMENT = 8
ROWS = 1024
NEAR_ROWS = ROWS // NEAR_DILATION
FAR_ROWS = ROWS // FAR_DILATION
QUARTER = ROWS // 4
QUARTER_PICKED = QUARTER // NEAR_DILATION + QUARTER // FAR_DILATION
PICKED = NEAR_ROWS + FAR_ROWS
SENT_ROWS = PICKED + PICKED // 2
PAIR = 2 * HEAD_DIM
NEG = -1e30
SCALE = HEAD_DIM ** -0.5
BF16 = jnp.bfloat16
F32 = jnp.float32
ROW_BLOCK = 128
VMEM_BYTES = 56 * 1024 * 1024
LESS_VMEM_BYTES = 20 * 1024 * 1024
SMALL = pl.CostEstimate(flops=1000, bytes_accessed=1000, transcendentals=0)


def lanes(shape):
    return lax.broadcasted_iota(jnp.int32, shape, 1)


def one_hot(offset_near, offset_far):
    row = lax.broadcasted_iota(jnp.int32, (QUARTER_PICKED, QUARTER), 0)
    col = lax.broadcasted_iota(jnp.int32, (QUARTER_PICKED, QUARTER), 1)
    count = QUARTER // NEAR_DILATION
    at = jnp.where(
        row < count,
        row * NEAR_DILATION + offset_near,
        (row - count) * FAR_DILATION + offset_far,
    )
    return jnp.where(col == at, 1.0, 0.0).astype(BF16)


def pick_kernel(offsets_ref, q_ref, k_ref, v_ref, out_ref):
    pair = pl.program_id(0)
    chosen = jnp.concatenate(
        [one_hot(offsets_ref[2 * pair + i, 0], offsets_ref[2 * pair + i, 1]) for i in range(2)], 0
    )
    split = QUARTER // NEAR_DILATION
    found = []
    for i in range(ROWS // QUARTER):
        block = slice(i * QUARTER, (i + 1) * QUARTER)
        fields = jnp.concatenate([q_ref[block, :], k_ref[block, :], v_ref[block, :]], 1)
        found.append(jnp.dot(chosen, fields, preferred_element_type=F32))
    low = lanes((PICKED, PAIR)) < HEAD_DIM
    for side in range(2):
        base = side * QUARTER_PICKED
        part = jnp.concatenate(
            [f[base : base + split] for f in found]
            + [f[base + split : base + QUARTER_PICKED] for f in found],
            0,
        )
        q, k, v = (part[:, i * PAIR : (i + 1) * PAIR] for i in range(3))
        if side == 0:
            kv = jnp.where(low, k, pltpu.roll(v, HEAD_DIM, 1))
        else:
            kv = jnp.where(low, pltpu.roll(k, HEAD_DIM, 1), v)
        other = pltpu.roll(q, HEAD_DIM, 1)
        q_low, q_high = (q, other) if side == 0 else (other, q)
        q_packed = []
        for start, count in ((0, NEAR_ROWS), (NEAR_ROWS, FAR_ROWS)):
            half = count // 2
            q_packed.append(
                jnp.where(
                    lanes((half, PAIR)) < HEAD_DIM,
                    q_low[start : start + half],
                    q_high[start + half : start + count],
                )
            )
        out_ref[side, 0:PICKED, :] = kv.astype(BF16)
        out_ref[side, PICKED:SENT_ROWS, :] = (jnp.concatenate(q_packed, 0) * SCALE).astype(BF16)


def pick(queries, keys, values, offsets):
    heads = queries.shape[1] // HEAD_DIM
    pair_spec = pl.BlockSpec((ROWS, PAIR), lambda i: (0, i))
    return pl.pallas_call(
        pick_kernel,
        grid=(heads // 2,),
        in_specs=[pl.BlockSpec(memory_space=pltpu.SMEM)] + [pair_spec] * 3,
        out_specs=pl.BlockSpec((2, SENT_ROWS, PAIR), lambda i: (i, 0, 0)),
        out_shape=jax.ShapeDtypeStruct((heads, SENT_ROWS, PAIR), BF16),
        compiler_params=pltpu.CompilerParams(vmem_limit_bytes=VMEM_BYTES),
        cost_estimate=SMALL,
        name="pick_rows",
    )(offsets, queries, keys, values)


def contract_lanes(a, b):
    return lax.dot_general(a, b, (((1,), (1,)), ((), ())), preferred_element_type=F32)


def with_ones(v):
    return jnp.concatenate([v, jnp.ones_like(v)], 1)


def softmax_sum(scores, values):
    peak = functools.reduce(jnp.maximum, [jnp.max(s, axis=1, keepdims=True) for s in scores])
    acc = None
    for s, v in zip(scores, values):
        part = jnp.dot(jnp.exp(s - peak).astype(BF16), v, preferred_element_type=F32)
        acc = part if acc is None else acc + part
    total = acc[:, PAIR:]
    return acc[:, :PAIR] / total, peak + jnp.log(total)


def local_kernel(q_ref, k_ref, v_ref, out_ref, lse_ref):
    keys = k_ref[...]
    values = with_ones(v_ref[...])
    low = lanes((ROW_BLOCK, PAIR)) < HEAD_DIM
    zero = jnp.zeros((), BF16)

    for i in range(ROWS // ROW_BLOCK):
        rows = pl.ds(i * ROW_BLOCK, ROW_BLOCK)
        q = q_ref[rows, :] * jnp.asarray(SCALE, BF16)
        both = [
            softmax_sum([contract_lanes(jnp.where(mine, q, zero), keys)], [values])
            for mine in (low, jnp.logical_not(low))
        ]
        out_ref[rows, :] = jnp.where(low, both[0][0], both[1][0]).astype(BF16)
        lse_ref[rows, :] = jnp.where(low, both[0][1], both[1][1])


def local_attention(queries, keys, values, first, count):
    spec = pl.BlockSpec((ROWS, PAIR), lambda i: (0, i + first))
    out_spec = pl.BlockSpec((ROWS, PAIR), lambda i: (0, i))
    return pl.pallas_call(
        local_kernel,
        grid=(count,),
        in_specs=[spec] * 3,
        out_specs=[out_spec] * 2,
        out_shape=[
            jax.ShapeDtypeStruct((ROWS, count * PAIR), BF16),
            jax.ShapeDtypeStruct((ROWS, count * PAIR), F32),
        ],
        compiler_params=pltpu.CompilerParams(vmem_limit_bytes=VMEM_BYTES),
        cost_estimate=SMALL,
        name="local_attention",
    )(queries, keys, values)


def unpack_queries(packed):
    low = lanes(packed.shape) < HEAD_DIM
    wide = packed.astype(F32)
    top = jnp.where(low, wide, 0.0).astype(BF16)
    bottom = jnp.where(low, pltpu.roll(wide, HEAD_DIM, 1), 0.0).astype(BF16)
    return top, bottom


def result_rows(out, lse):
    high = lse.astype(BF16)
    rest = (lse - high.astype(F32)).astype(BF16)
    lane = lanes(out.shape)
    moved = pltpu.roll(out, HEAD_DIM, 1)
    stats = jnp.where(lane < HEAD_DIM + HEAD_DIM // 2, high.astype(F32), rest.astype(F32))
    return jnp.where(lane < HEAD_DIM, moved, stats).astype(BF16)


def near_kernel(sent_ref, out_ref):
    near_kv = jnp.concatenate([sent_ref[i, 0:NEAR_ROWS, :] for i in range(SEGMENT)], 0)
    near_values = with_ones(near_kv)
    half = NEAR_ROWS // 2
    for i in range(SEGMENT):
        q = jnp.concatenate(unpack_queries(sent_ref[i, PICKED : PICKED + half, :]), 0)
        out_ref[i] = result_rows(*softmax_sum([contract_lanes(q, near_kv)], [near_values]))


def far_kernel(sent_ref, far0_ref, far1_ref, far2_ref, far3_ref, out_ref):
    far = [r[...] for r in (far0_ref, far1_ref, far2_ref, far3_ref)]
    far_values = [with_ones(f) for f in far]
    half = FAR_ROWS // 2
    for i in range(SEGMENT // 2):
        packed = jnp.concatenate(
            [sent_ref[2 * i + j, SENT_ROWS - half : SENT_ROWS, :] for j in range(2)], 0
        )
        q = jnp.concatenate(unpack_queries(packed), 0)
        res = result_rows(*softmax_sum([contract_lanes(q, f) for f in far], far_values))
        for j in range(2):
            out_ref[2 * i + j, 0:half, :] = res[j * half : (j + 1) * half]
            out_ref[2 * i + j, half:FAR_ROWS, :] = res[(2 + j) * half : (3 + j) * half]


def near_attention(sent):
    return pl.pallas_call(
        near_kernel,
        in_specs=[pl.BlockSpec(memory_space=pltpu.VMEM)],
        out_specs=pl.BlockSpec(memory_space=pltpu.VMEM),
        out_shape=jax.ShapeDtypeStruct((SEGMENT, NEAR_ROWS, PAIR), BF16),
        compiler_params=pltpu.CompilerParams(vmem_limit_bytes=LESS_VMEM_BYTES),
        cost_estimate=SMALL,
        name="near_attention",
    )(sent)


def far_attention(sent, far):
    return pl.pallas_call(
        far_kernel,
        in_specs=[pl.BlockSpec(memory_space=pltpu.VMEM)] * 5,
        out_specs=pl.BlockSpec(memory_space=pltpu.VMEM),
        out_shape=jax.ShapeDtypeStruct((SEGMENT, FAR_ROWS, PAIR), BF16),
        compiler_params=pltpu.CompilerParams(vmem_limit_bytes=LESS_VMEM_BYTES),
        cost_estimate=SMALL,
        name="far_attention",
    )(sent, *far)


def combine_kernel(quarter_ref, offsets_ref, out_ref, lse_ref, out2_ref, lse2_ref, near_ref, far_ref, attn_ref):
    quarter = quarter_ref[0]
    low_rows = lanes((QUARTER, PAIR)) < HEAD_DIM
    position = lax.broadcasted_iota(jnp.int32, (QUARTER, PAIR), 0) + quarter * QUARTER
    early = out_ref.shape[1] // PAIR
    for pair in range(attn_ref.shape[1] // PAIR):
        columns = slice(pair * PAIR, (pair + 1) * PAIR)
        if pair < early:
            outs, lses = [out_ref[:, columns].astype(F32)], [lse_ref[:, columns]]
        else:
            late = slice((pair - early) * PAIR, (pair - early + 1) * PAIR)
            outs, lses = [out2_ref[:, late].astype(F32)], [lse2_ref[:, late]]
        for which, (back_ref, dilation) in enumerate(
            ((near_ref, NEAR_DILATION), (far_ref, FAR_DILATION))
        ):
            count = QUARTER // dilation
            rows = pl.ds(pl.multiple_of(quarter * count, count), count)
            offset = [offsets_ref[2 * pair + side, which] for side in range(2)]
            row = lax.broadcasted_iota(jnp.int32, (QUARTER, 2 * count), 0)
            col = lax.broadcasted_iota(jnp.int32, (QUARTER, 2 * count), 1)
            at = jnp.where(
                col < count, col * dilation + offset[0], (col - count) * dilation + offset[1]
            )
            placed = jnp.where(row == at, 1.0, 0.0).astype(BF16)
            low = lanes((count, PAIR)) < HEAD_DIM
            first = back_ref[2 * pair, rows, :].astype(F32)
            second = back_ref[2 * pair + 1, rows, :].astype(F32)
            zero = jnp.zeros((count, PAIR), F32)
            top = jnp.concatenate(
                [
                    jnp.where(low, first, zero),
                    jnp.where(low, first[:, 64:65], zero),
                    jnp.where(low, first[:, 96:97], zero),
                ],
                1,
            )
            bottom = jnp.concatenate(
                [
                    jnp.where(low, zero, pltpu.roll(second, HEAD_DIM, 1)),
                    jnp.where(low, zero, second[:, 64:65]),
                    jnp.where(low, zero, second[:, 96:97]),
                ],
                1,
            )
            wide = jnp.dot(
                placed, jnp.concatenate([top, bottom], 0).astype(BF16), preferred_element_type=F32
            )
            here = jnp.where(low_rows, offset[0], offset[1])
            hit = (position & (dilation - 1)) == here
            outs.append(wide[:, :PAIR])
            lses.append(jnp.where(hit, wide[:, PAIR : 2 * PAIR] + wide[:, 2 * PAIR :], NEG))
        peak = jnp.maximum(jnp.maximum(lses[0], lses[1]), lses[2])
        numer, denom = 0.0, 0.0
        for out, lse in zip(outs, lses):
            weight = jnp.exp(lse - peak)
            numer = numer + weight * out
            denom = denom + weight
        attn_ref[:, columns] = (numer / denom).astype(BF16)


def combine(quarter, offsets, local_parts, near, far):
    blocks = [
        pl.BlockSpec((QUARTER, part.shape[1]), lambda i, quarter: (quarter[0], 0))
        for part in local_parts
    ]
    whole = [pl.BlockSpec(memory_space=pltpu.VMEM)] * 2
    width = sum(part.shape[1] for part in local_parts[::2])
    return pl.pallas_call(
        combine_kernel,
        grid_spec=pltpu.PrefetchScalarGridSpec(
            num_scalar_prefetch=1,
            grid=(1,),
            in_specs=[pl.BlockSpec(memory_space=pltpu.SMEM)] + blocks + whole,
            out_specs=pl.BlockSpec((QUARTER, width), lambda i, quarter: (0, 0)),
        ),
        out_shape=jax.ShapeDtypeStruct((QUARTER, width), BF16),
        compiler_params=pltpu.CompilerParams(vmem_limit_bytes=LESS_VMEM_BYTES),
        cost_estimate=SMALL,
        name="combine_patterns",
    )(quarter.reshape(1), offsets, *local_parts, near, far)


def project_kernel(has_base, *refs):
    out_ref = refs[-1]
    base_ref = refs[0] if has_base else None
    terms = refs[1:-1] if has_base else refs[:-1]
    width = 512
    for start in range(0, out_ref.shape[1], width):
        columns = slice(start, start + width)
        total = base_ref[:, columns] if has_base else None
        for rows_ref, first, weight_ref in zip(terms[0::2], (0, 256) * 4, terms[1::2]):
            rows = rows_ref[...]
            depth = weight_ref.shape[0]
            if depth < rows.shape[1]:
                rows = rows[:, first : first + depth]
            part = jnp.dot(rows, weight_ref[:, columns], preferred_element_type=F32)
            total = part if total is None else total + part
        out_ref[:, columns] = total.astype(out_ref.dtype)


def project(base, terms, dtype):
    operands = ([] if base is None else [base]) + [x for term in terms for x in term]
    width = terms[0][1].shape[1]
    return pl.pallas_call(
        functools.partial(project_kernel, base is not None),
        in_specs=[pl.BlockSpec(memory_space=pltpu.VMEM)] * len(operands),
        out_specs=pl.BlockSpec(memory_space=pltpu.VMEM),
        out_shape=jax.ShapeDtypeStruct((QUARTER, width), dtype),
        compiler_params=pltpu.CompilerParams(vmem_limit_bytes=LESS_VMEM_BYTES),
        cost_estimate=SMALL,
        name="project",
    )(*operands)


def swap(shard, axis, bits):
    return lax.ppermute(shard, axis, [(i, i ^ bits) for i in range(lax.axis_size(axis))])


def local(queries, keys, values, offsets, out_weight):
    heads = queries.shape[1] // HEAD_DIM
    place = lax.axis_index("tp")
    mine = lax.dynamic_slice_in_dim(offsets, place * heads, heads, 0)
    mine = jnp.stack([mine[:, 0] % NEAR_DILATION, mine[:, 1] % FAR_DILATION], 1)
    n_tp, n_ctx = lax.axis_size("tp"), lax.axis_size("ctx")

    picked = pick(queries, keys, values, mine)
    picked, sent_weight = lax.optimization_barrier((picked, out_weight))
    segments = [[s * SEGMENT + i for i in range(SEGMENT)] for s in range(n_ctx // SEGMENT)]
    sent = lax.all_to_all(picked, "ctx", 0, 0, axis_index_groups=segments, tiled=True)
    other = [(c * n_tp + t, (c ^ 1) * n_tp + (t ^ 2)) for c in range(n_ctx) for t in range(n_tp)]
    cut = out_weight.shape[0] // 2
    weight_2 = [
        swap(sent_weight[:cut], "tp", 2),
        lax.ppermute(sent_weight[cut:], ("ctx", "tp"), other),
    ]
    weight_1 = swap(sent_weight, "tp", 1)
    early = local_attention(queries, keys, values, 0, 3)
    sent, early, weight_1 = lax.optimization_barrier((sent, early, weight_1))

    far_kv = sent[:, NEAR_ROWS:PICKED, :].reshape(SEGMENT * FAR_ROWS, PAIR)
    far_kv = jnp.concatenate([far_kv, swap(far_kv, "ctx", 8)], 0)
    near_back = near_attention(sent)
    far_kv, near_back, queries = lax.optimization_barrier((far_kv, near_back, queries))
    far = [far_kv] + [swap(far_kv, "ctx", 16 * i) for i in (1, 2, 3)]
    late = local_attention(queries, keys, values, 3, 1)
    far, late, weight_2 = lax.optimization_barrier((far, late, weight_2))
    weight_3 = [swap(w, "tp", 1) for w in weight_2]

    back = jnp.concatenate([near_back, far_attention(sent, far)], 1)
    back = lax.all_to_all(back, "ctx", 0, 0, axis_index_groups=segments, tiled=True)
    near_rows, far_rows = back[:, :NEAR_ROWS], back[:, NEAR_ROWS:]
    local_parts = [*early, *late]
    away = [combine(place ^ i, mine, local_parts, near_rows, far_rows) for i in (3, 2)]
    came_3, came_2 = (swap(rows, "tp", i) for rows, i in zip(away, (3, 2)))
    near_rows, far_rows, _ = lax.optimization_barrier((near_rows, far_rows, away))
    came_1 = swap(combine(place ^ 1, mine, local_parts, near_rows, far_rows), "tp", 1)
    own = combine(place, mine, local_parts, near_rows, far_rows)
    base = project(None, [(own, out_weight), (came_1, weight_1)], F32)
    terms = [(came_2, w) for w in weight_2] + [(came_3, w) for w in weight_3]
    return project(base, terms, BF16)


def solution(mesh):
    return jax.shard_map(
        local,
        mesh=mesh,
        in_specs=(P("ctx", "tp"), P("ctx", "tp"), P("ctx", "tp"), P(), P("tp", None)),
        out_specs=P(("ctx", "tp"), None),
        check_vma=False,
    )
```

time: 128 us -> 108 us (0.84)
  blocking collectives: 26.1 us -> 0 us
  starting transfers between devices: 20.7 us -> 35.7 us
  local copies, waits for them, and re-layouts: 12.9 us -> 4.81 us
  waiting for transfers between devices: 20.3 us -> 26.8 us
  matrix products: 4.18 us -> 0 us
  other arithmetic: 2.92 us -> 0.82 us
    all_to_all x1 -> x0, blocking collectives: 26.1 us -> none  [local(): lax.all_to_all(picked, 'ctx', 0, 0, axis_index_groups=segments, tiled=True)]
    all_to_all x1, waiting for transfers between devices: 0.01 us -> 11 us  [local(): lax.all_to_all(back, 'ctx', 0, 0, axis_index_groups=segments, tiled=True)]
    unnamed x24 -> x16, local copies, waits for them, and re-layouts: 10.9 us -> 0.71 us
    ppermute x7 -> x11, waiting for transfers between devices: 20.3 us -> 13.6 us  [swap(): lax.ppermute(shard, axis, [(i, i ^ bits) for i in range(lax.axis_size(axi...]
    all_to_all x0 -> x1, starting transfers between devices: none -> 6.51 us  [local(): lax.all_to_all(picked, 'ctx', 0, 0, axis_index_groups=segments, tiled=True)]
    ppermute x7 -> x11, starting transfers between devices: 12.6 us -> 17.5 us  [swap(): lax.ppermute(shard, axis, [(i, i ^ bits) for i in range(lax.axis_size(axi...]
    dot_general x2 -> x0, matrix products: 4.18 us -> none  [the longest x1 2.83 us: local(): jnp.dot(came, weight_there, preferred_element_type=F32)]
    convert_element_type x1 -> x0, other arithmetic: 2.88 us -> none  [local(): return (keep + swap(give, 'tp', 1).astype(F32)).astype(BF16)]
  transfers between devices with their start and end apart: 9 -> 14, of which waited for: 6 -> 7; matrix products, arithmetic and copies ran while one was open for 1% -> 4% of each run, Pallas kernels for 28% -> 28%
where the time goes in v2:
time: 108 us; the launch traced here: 107 us
  Pallas kernels  39.2 us (36%)
  starting transfers between devices  35.7 us (33%)
  waiting for transfers between devices  26.8 us (25%)
  local copies, waits for them, and re-layouts  4.81 us (4%)
    ppermute x11, starting transfers between devices, swap(): lax.ppermute(shard, axis, [(i, i ^ bits) for i in range(lax.axis_size(axi...  17.5 us
    pallas_call x2, Pallas kernels, local_attention(): pl.pallas_call(local_kernel, grid=(count,), in_specs=[spec] * 3, out_spec...  15.3 us
    ppermute x11, waiting for transfers between devices, swap(): lax.ppermute(shard, axis, [(i, i ^ bits) for i in range(lax.axis_size(axi...  13.6 us
    all_to_all x1, waiting for transfers between devices, local(): lax.all_to_all(back, 'ctx', 0, 0, axis_index_groups=segments, tiled=True)  11 us
    all_to_all x1, starting transfers between devices, local(): lax.all_to_all(back, 'ctx', 0, 0, axis_index_groups=segments, tiled=True)  8.94 us
    pallas_call x2, Pallas kernels, project(): pl.pallas_call(functools.partial(project_kernel, base is not None), in_sp...  7.32 us
    all_to_all x1, starting transfers between devices, local(): lax.all_to_all(picked, 'ctx', 0, 0, axis_index_groups=segments, tiled=True)  6.51 us
    pallas_call x4, Pallas kernels, combine(): pl.pallas_call(combine_kernel, grid_spec=pltpu.PrefetchScalarGridSpec(num...  6.12 us
  transfers between devices with their start and end apart: 14, of which 7 were waited for; matrix products, arithmetic and copies ran while one was open for 4% of the time, Pallas kernels for 28%

profile of v2, /device:TPU:1, one launch (start us, length us, event | category | flops | bytes accessed | tf_op | source)
XLA Modules:
  0.0 107.5 jit_solution(10751282123492175479)
XLA Ops:
  0.0 0.7 copy-done
  0.7 0.1 constant_dynamic-slice_fusion
  0.8 0.7 copy.10.offsets_ref
  1.5 4.3 %pick_rows.1 = bf16[8,288,128]{2,1,0:T(8,128)(2,1)} custom-call(s32[8,2]{1,0:T(8,128)} %copy.10.offsets_ref, bf16[1024,512]{1,0:T(8,128)(2,1)} %q_ref.4, bf16[1024,512]{1,0:T(8,128)(2,1)} %k_ref.5, bf16[1024,512]{1,0:T(8,128)(2,1)} %v_ref.5), custom_call_target="tpu_custom_call" | custom-call | flops 1000 | bytes 1000 | tf_op jit(solution)/shard_map/pick_rows/pallas_call | solution.py:91
  5.8 3.2 %collective-permute-start = (bf16[512,2048]{1,0:T(8,128)(2,1)S(1)}, bf16[512,2048]{1,0:T(8,128)(2,1)}, u32[]{:S(2)}, u32[]{:S(2)}) collective-permute-start(bf16[512,2048]{1,0:T(8,128)(2,1)S(1)} %copy-done.4), channel_id=1, source_target_pairs={{0,1},{1,0},{2,3},{3,2},{4,5},{5,4},{6,7},{7,6},{8,9},{9,8},{10,11... | collective-permute-start | bytes 6291464 | tf_op jit(solution)/shard_map/ppermute | solution.py:336
  9.0 6.5 %all-to-all-start = ((bf16[8,288,128]{2,1,0:T(8,128)(2,1)}), bf16[8,288,128]{2,1,0:T(8,128)(2,1)S(1)}, u32[]{:S(2)}, u32[]{:S(2)}) async-start(bf16[8,288,128]{2,1,0:T(8,128)(2,1)} %pick_rows.1), calls=%async_computation | async-start | bytes 1179648 | tf_op jit(solution)/shard_map/all_to_all | solution.py:349
  15.5 1.5 %fusion.2 = (bf16[256,2048]{1,0:T(8,128)(2,1)}, bf16[256,2048]{1,0:T(8,128)(2,1)}) fusion(bf16[512,2048]{1,0:T(8,128)(2,1)S(1)} %copy-done.4), kind=kLoop, calls=%fused_computation.12 | loop fusion | bytes 4194304 | tf_op jit(solution)/shard_map/slice | solution.py:354
  17.0 2.8 %collective-permute-start.6 = (bf16[256,2048]{1,0:T(8,128)(2,1)}, bf16[256,2048]{1,0:T(8,128)(2,1)}, u32[]{:S(2)}, u32[]{:S(2)}) collective-permute-start(bf16[256,2048]{1,0:T(8,128)(2,1)} %get-tuple-element.51), channel_id=1, source_target_pairs={{0,6},{1,7},{2,4},{3,5},{4,2},{5,3},{6,0},{7,1},{8,14},{9,15},{10,... | collective-permute-start | bytes 3145736 | tf_op jit(solution)/shard_map/ppermute | solution.py:354
  19.8 0.0 collective-permute-start.5
  19.8 10.5 %local_attention.2 = (bf16[1024,384]{1,0:T(8,128)(2,1)}, f32[1024,384]{1,0:T(8,128)}) custom-call(bf16[1024,512]{1,0:T(8,128)(2,1)} %q_ref.4, bf16[1024,512]{1,0:T(8,128)(2,1)} %k_ref.5, bf16[1024,512]{1,0:T(8,128)(2,1)} %v_ref.5), custom_call_target="tpu_custom_call" | custom-call | flops 1000 | bytes 1000 | tf_op jit(solution)/shard_map/local_attention/pallas_call | solution.py:141
  30.3 1.1 %all-to-all-done.sent_ref = bf16[8,288,128]{2,1,0:T(8,128)(2,1)S(1)} async-done(((bf16[8,288,128]{2,1,0:T(8,128)(2,1)}), bf16[8,288,128]{2,1,0:T(8,128)(2,1)S(1)}, u32[]{:S(2)}, u32[]{:S(2)}) %all-to-all-start) | async-done | bytes 589856 | tf_op jit(solution)/shard_map/all_to_all | solution.py:349
  31.4 0.0 collective-permute-done.refs_3_
  31.4 4.3 %collective-permute-start.1 = (bf16[512,128]{1,0:T(8,128)(2,1)S(1)}, bf16[512,128]{1,0:T(8,128)(2,1)S(1)}, u32[]{:S(2)}, u32[]{:S(2)}) collective-permute-start(bf16[512,128]{1,0:T(8,128)(2,1)S(1)} %bitcast.5), channel_id=1, source_target_pairs={{0,32},{4,36},{8,40},{12,44},{16,48},{20,52},{24,56},{28,60},{32,0... | collective-permute-start | bytes 393224 | tf_op jit(solution)/shard_map/ppermute | solution.py:336
  35.7 1.9 %near_attention.1 = bf16[8,128,128]{2,1,0:T(8,128)(2,1)S(1)} custom-call(bf16[8,288,128]{2,1,0:T(8,128)(2,1)S(1)} %all-to-all-done.sent_ref), custom_call_target="tpu_custom_call" | custom-call | flops 1000 | bytes 1000 | tf_op jit(solution)/shard_map/near_attention/pallas_call | solution.py:198
  37.6 1.7 %collective-permute-done.1 = bf16[512,128]{1,0:T(8,128)(2,1)S(1)} collective-permute-done((bf16[512,128]{1,0:T(8,128)(2,1)S(1)}, bf16[512,128]{1,0:T(8,128)(2,1)S(1)}, u32[]{:S(2)}, u32[]{:S(2)}) %collective-permute-start.1) | collective-permute-done | bytes 131104 | tf_op jit(solution)/shard_map/ppermute | solution.py:336
  39.3 2.6 %collective-permute-start.4 = (bf16[1024,128]{1,0:T(8,128)(2,1)S(1)}, bf16[1024,128]{1,0:T(8,128)(2,1)S(1)}, u32[]{:S(2)}, u32[]{:S(2)}) collective-permute-start(bf16[1024,128]{1,0:T(8,128)(2,1)S(1)} %pad_maximum_fusion.1.far0_ref), channel_id=1, source_target_pairs={{0,192},{4,196},{8,200},{12,204},{16,208},{20,212},{24,216},{28,22... | collective-permute-start | bytes 786440 | tf_op jit(solution)/shard_map/ppermute | solution.py:336
  41.9 0.5 collective-permute-start.3
  42.4 0.3 collective-permute-start.2
  42.7 4.8 %local_attention.3 = (bf16[1024,128]{1,0:T(8,128)(2,1)}, f32[1024,128]{1,0:T(8,128)}) custom-call(bf16[1024,512]{1,0:T(8,128)(2,1)} %q_ref.4, bf16[1024,512]{1,0:T(8,128)(2,1)} %k_ref.5, bf16[1024,512]{1,0:T(8,128)(2,1)} %v_ref.5), custom_call_target="tpu_custom_call" | custom-call | flops 1000 | bytes 1000 | tf_op jit(solution)/shard_map/local_attention/pallas_call | solution.py:141
  47.5 1.1 collective-permute-done.6.refs_4_
  48.6 0.0 collective-permute-done.5.refs_2_
  48.6 4.4 %collective-permute-done.4.far3_ref = bf16[1024,128]{1,0:T(8,128)(2,1)S(1)} collective-permute-done((bf16[1024,128]{1,0:T(8,128)(2,1)S(1)}, bf16[1024,128]{1,0:T(8,128)(2,1)S(1)}, u32[]{:S(2)}, u32[]{:S(2)}) %collective-permute-start.4) | collective-permute-done | bytes 262176 | tf_op jit(solution)/shard_map/ppermute | solution.py:336
  53.0 0.0 collective-permute-done.3.far2_ref
  53.0 0.0 collective-permute-done.2.far1_ref
  53.0 2.6 %collective-permute-start.10 = (bf16[256,2048]{1,0:T(8,128)(2,1)}, bf16[256,2048]{1,0:T(8,128)(2,1)}, u32[]{:S(2)}, u32[]{:S(2)}) collective-permute-start(bf16[256,2048]{1,0:T(8,128)(2,1)} %collective-permute-done.5.refs_2_), channel_id=1, source_target_pairs={{0,1},{1,0},{2,3},{3,2},{4,5},{5,4},{6,7},{7,6},{8,9},{9,8},{10,11... | collective-permute-start | bytes 3145736 | tf_op jit(solution)/shard_map/ppermute | solution.py:336
  55.6 0.0 collective-permute-start.11
  55.6 4.2 %far_attention.1 = bf16[8,64,128]{2,1,0:T(8,128)(2,1)S(1)} custom-call(bf16[8,288,128]{2,1,0:T(8,128)(2,1)S(1)} %all-to-all-done.sent_ref, bf16[1024,128]{1,0:T(8,128)(2,1)S(1)} %pad_maximum_fusion.1.far0_ref, bf16[1024,128]{1,0:T(8,128)(2,1)S(1)} %collective-permute-done.2.far1_ref, bf16[1024,128]{1,0:T(8,128)(2,1)S(1)} %collective-permute-done.3.far2_ref, ...), custom_call_target="tpu_custom_call" | custom-call | flops 1000 | bytes 1000 | tf_op jit(solution)/shard_map/far_attention/pallas_call | solution.py:210
  59.8 0.0 copy-start.6
  59.8 0.8 pad_maximum_fusion
  60.6 8.9 %all-to-all-start.1 = ((bf16[8,192,128]{2,1,0:T(8,128)(2,1)}), bf16[8,192,128]{2,1,0:T(8,128)(2,1)}, u32[]{:S(2)}, u32[]{:S(2)}) async-start(bf16[8,192,128]{2,1,0:T(8,128)(2,1)} %pad_maximum_fusion), calls=%async_computation.1 | async-start | bytes 786432 | tf_op jit(solution)/shard_map/all_to_all | solution.py:370
  69.5 11.0 %all-to-all-done.1 = bf16[8,192,128]{2,1,0:T(8,128)(2,1)} async-done(((bf16[8,192,128]{2,1,0:T(8,128)(2,1)}), bf16[8,192,128]{2,1,0:T(8,128)(2,1)}, u32[]{:S(2)}, u32[]{:S(2)}) %all-to-all-start.1) | async-done | bytes 393248 | tf_op jit(solution)/shard_map/all_to_all | solution.py:370
  80.5 0.9 slice.29.far_ref
  81.5 1.0 slice.28.near_ref
  82.5 1.5 %combine_patterns.5 = bf16[256,512]{1,0:T(8,128)(2,1)S(1)} custom-call(s32[1]{0:T(128)} %bitcast.3.quarter_ref, s32[8,2]{1,0:T(8,128)S(1)} %copy-done.7, bf16[1024,384]{1,0:T(8,128)(2,1)S(1)} %copy-done.2, f32[1024,384]{1,0:T(8,128)S(1)} %copy-done.1, bf16[1024,128]{1,0:T(8,128)(2,1)S(1)} %copy-done.6, f32[1024,128]{1,0:T(8,128)S(1)} %copy-done.3, ...), custom_call_target="tpu_custom_call" | custom-call | flops 1000 | bytes 1000 | tf_op jit(solution)/shard_map/combine_patterns/pallas_call | solution.py:288
  84.0 1.5 %combine_patterns.4 = bf16[256,512]{1,0:T(8,128)(2,1)S(1)} custom-call(s32[1]{0:T(128)} %bitcast.2.quarter_ref, s32[8,2]{1,0:T(8,128)S(1)} %copy-done.7, bf16[1024,384]{1,0:T(8,128)(2,1)S(1)} %copy-done.2, f32[1024,384]{1,0:T(8,128)S(1)} %copy-done.1, bf16[1024,128]{1,0:T(8,128)(2,1)S(1)} %copy-done.6, f32[1024,128]{1,0:T(8,128)S(1)} %copy-done.3, ...), custom_call_target="tpu_custom_call" | custom-call | flops 1000 | bytes 1000 | tf_op jit(solution)/shard_map/combine_patterns/pallas_call | solution.py:288
  85.6 1.5 %combine_patterns.7 = bf16[256,512]{1,0:T(8,128)(2,1)S(1)} custom-call(s32[1]{0:T(128)} %bitcast.4.quarter_ref, s32[8,2]{1,0:T(8,128)S(1)} %copy-done.7, bf16[1024,384]{1,0:T(8,128)(2,1)S(1)} %copy-done.2, f32[1024,384]{1,0:T(8,128)S(1)} %copy-done.1, bf16[1024,128]{1,0:T(8,128)(2,1)S(1)} %copy-done.6, f32[1024,128]{1,0:T(8,128)S(1)} %copy-done.3, ...), custom_call_target="tpu_custom_call" | custom-call | flops 1000 | bytes 1000 | tf_op jit(solution)/shard_map/combine_patterns/pallas_call | solution.py:288
  87.1 0.0 copy-start.5
  87.1 2.5 %collective-permute-start.7 = (bf16[256,512]{1,0:T(8,128)(2,1)S(1)}, bf16[256,512]{1,0:T(8,128)(2,1)S(1)}, u32[]{:S(2)}, u32[]{:S(2)}) collective-permute-start(bf16[256,512]{1,0:T(8,128)(2,1)S(1)} %combine_patterns.7), channel_id=1, source_target_pairs={{0,1},{1,0},{2,3},{3,2},{4,5},{5,4},{6,7},{7,6},{8,9},{9,8},{10,11... | collective-permute-start | bytes 786440 | tf_op jit(solution)/shard_map/ppermute | solution.py:336
  89.6 0.6 collective-permute-start.9
  90.2 0.8 collective-permute-start.8
  91.1 1.5 %combine_patterns.6.refs_0_ = bf16[256,512]{1,0:T(8,128)(2,1)S(1)} custom-call(s32[1]{0:T(128)} %bitcast.quarter_ref, s32[8,2]{1,0:T(8,128)S(1)} %copy-done.7, bf16[1024,384]{1,0:T(8,128)(2,1)S(1)} %copy-done.2, f32[1024,384]{1,0:T(8,128)S(1)} %copy-done.1, bf16[1024,128]{1,0:T(8,128)(2,1)S(1)} %copy-done.6, f32[1024,128]{1,0:T(8,128)S(1)} %copy-done.3, ...), custom_call_target="tpu_custom_call" | custom-call | flops 1000 | bytes 1000 | tf_op jit(solution)/shard_map/combine_patterns/pallas_call | solution.py:288
  92.6 0.0 collective-permute-done.7.refs_2_
  92.6 2.9 %project.2.refs_0_ = f32[256,2048]{1,0:T(8,128)S(1)} custom-call(bf16[256,512]{1,0:T(8,128)(2,1)S(1)} %combine_patterns.6.refs_0_, bf16[512,2048]{1,0:T(8,128)(2,1)S(1)} %copy-done.5, bf16[256,512]{1,0:T(8,128)(2,1)S(1)} %collective-permute-done.7.refs_2_, bf16[512,2048]{1,0:T(8,128)(2,1)} %collective-permute-done.refs_3_), custom_call_target="tpu_custom_call" | custom-call | flops 1000 | bytes 1000 | tf_op jit(solution)/shard_map/project/pallas_call | solution.py:324
  95.5 2.7 %collective-permute-done.9.refs_5_.refs_7_ = bf16[256,512]{1,0:T(8,128)(2,1)S(1)} collective-permute-done((bf16[256,512]{1,0:T(8,128)(2,1)S(1)}, bf16[256,512]{1,0:T(8,128)(2,1)S(1)}, u32[]{:S(2)}, u32[]{:S(2)}) %collective-permute-start.9) | collective-permute-done | bytes 262176 | tf_op jit(solution)/shard_map/ppermute | solution.py:336
  98.2 4.8 %collective-permute-done.8.refs_1_.refs_3_ = bf16[256,512]{1,0:T(8,128)(2,1)S(1)} collective-permute-done((bf16[256,512]{1,0:T(8,128)(2,1)S(1)}, bf16[256,512]{1,0:T(8,128)(2,1)S(1)}, u32[]{:S(2)}, u32[]{:S(2)}) %collective-permute-start.8) | collective-permute-done | bytes 262176 | tf_op jit(solution)/shard_map/ppermute | solution.py:336
  103.0 0.0 collective-permute-done.10.refs_6_
  103.0 0.0 collective-permute-done.11.refs_8_
  103.0 4.5 %project.3 = bf16[256,2048]{1,0:T(8,128)(2,1)} custom-call(f32[256,2048]{1,0:T(8,128)S(1)} %project.2.refs_0_, bf16[256,512]{1,0:T(8,128)(2,1)S(1)} %collective-permute-done.8.refs_1_.refs_3_, bf16[256,2048]{1,0:T(8,128)(2,1)} %collective-permute-done.5.refs_2_, bf16[256,512]{1,0:T(8,128)(2,1)S(1)} %collective-permute-done.8.refs_1_.refs_3_, ...), custom_call_target="tpu_custom_call" | custom-call | flops 1000 | bytes 1000 | tf_op jit(solution)/shard_map/project/pallas_call | solution.py:324
  (17 shorter events, 0.1 us)
Async XLA Ops:
  0.0 0.7 copy-start
  0.0 5.8 %copy-start.4 = (bf16[512,2048]{1,0:T(8,128)(2,1)S(1)}, bf16[512,2048]{1,0:T(8,128)(2,1)}, u32[]{:S(2)}) copy-start(bf16[512,2048]{1,0:T(8,128)(2,1)} %refs_1_.1) | copy-start | bytes 6291460
  5.8 25.6 %collective-permute-start = (bf16[512,2048]{1,0:T(8,128)(2,1)S(1)}, bf16[512,2048]{1,0:T(8,128)(2,1)}, u32[]{:S(2)}, u32[]{:S(2)}) collective-permute-start(bf16[512,2048]{1,0:T(8,128)(2,1)S(1)} %copy-done.4), channel_id=1, source_target_pairs={{0,1},{1,0},{2,3},{3,2},{4,5},{5,4},{6,7},{7,6},{8,9},{9,8},{10,11... | collective-permute-start | bytes 6291464 | tf_op jit(solution)/shard_map/ppermute | solution.py:336
  9.0 22.3 %all-to-all-start = ((bf16[8,288,128]{2,1,0:T(8,128)(2,1)}), bf16[8,288,128]{2,1,0:T(8,128)(2,1)S(1)}, u32[]{:S(2)}, u32[]{:S(2)}) async-start(bf16[8,288,128]{2,1,0:T(8,128)(2,1)} %pick_rows.1), calls=%async_computation | async-start | bytes 1179648 | tf_op jit(solution)/shard_map/all_to_all | solution.py:349
  17.0 31.6 %collective-permute-start.6 = (bf16[256,2048]{1,0:T(8,128)(2,1)}, bf16[256,2048]{1,0:T(8,128)(2,1)}, u32[]{:S(2)}, u32[]{:S(2)}) collective-permute-start(bf16[256,2048]{1,0:T(8,128)(2,1)} %get-tuple-element.51), channel_id=1, source_target_pairs={{0,6},{1,7},{2,4},{3,5},{4,2},{5,3},{6,0},{7,1},{8,14},{9,15},{10,... | collective-permute-start | bytes 3145736 | tf_op jit(solution)/shard_map/ppermute | solution.py:354
  19.8 28.8 %collective-permute-start.5 = (bf16[256,2048]{1,0:T(8,128)(2,1)}, bf16[256,2048]{1,0:T(8,128)(2,1)}, u32[]{:S(2)}, u32[]{:S(2)}) collective-permute-start(bf16[256,2048]{1,0:T(8,128)(2,1)} %get-tuple-element.52), channel_id=1, source_target_pairs={{0,2},{1,3},{2,0},{3,1},{4,6},{5,7},{6,4},{7,5},{8,10},{9,11},{10,... | collective-permute-start | bytes 3145736 | tf_op jit(solution)/shard_map/ppermute | solution.py:336
  31.4 7.9 %collective-permute-start.1 = (bf16[512,128]{1,0:T(8,128)(2,1)S(1)}, bf16[512,128]{1,0:T(8,128)(2,1)S(1)}, u32[]{:S(2)}, u32[]{:S(2)}) collective-permute-start(bf16[512,128]{1,0:T(8,128)(2,1)S(1)} %bitcast.5), channel_id=1, source_target_pairs={{0,32},{4,36},{8,40},{12,44},{16,48},{20,52},{24,56},{28,60},{32,0... | collective-permute-start | bytes 393224 | tf_op jit(solution)/shard_map/ppermute | solution.py:336
  39.3 13.7 %collective-permute-start.4 = (bf16[1024,128]{1,0:T(8,128)(2,1)S(1)}, bf16[1024,128]{1,0:T(8,128)(2,1)S(1)}, u32[]{:S(2)}, u32[]{:S(2)}) collective-permute-start(bf16[1024,128]{1,0:T(8,128)(2,1)S(1)} %pad_maximum_fusion.1.far0_ref), channel_id=1, source_target_pairs={{0,192},{4,196},{8,200},{12,204},{16,208},{20,212},{24,216},{28,22... | collective-permute-start | bytes 786440 | tf_op jit(solution)/shard_map/ppermute | solution.py:336
  41.9 11.1 %collective-permute-start.3 = (bf16[1024,128]{1,0:T(8,128)(2,1)S(1)}, bf16[1024,128]{1,0:T(8,128)(2,1)S(1)}, u32[]{:S(2)}, u32[]{:S(2)}) collective-permute-start(bf16[1024,128]{1,0:T(8,128)(2,1)S(1)} %pad_maximum_fusion.1.far0_ref), channel_id=1, source_target_pairs={{0,128},{4,132},{8,136},{12,140},{16,144},{20,148},{24,152},{28,15... | collective-permute-start | bytes 786440 | tf_op jit(solution)/shard_map/ppermute | solution.py:336
  42.4 10.6 %collective-permute-start.2 = (bf16[1024,128]{1,0:T(8,128)(2,1)S(1)}, bf16[1024,128]{1,0:T(8,128)(2,1)S(1)}, u32[]{:S(2)}, u32[]{:S(2)}) collective-permute-start(bf16[1024,128]{1,0:T(8,128)(2,1)S(1)} %pad_maximum_fusion.1.far0_ref), channel_id=1, source_target_pairs={{0,64},{4,68},{8,72},{12,76},{16,80},{20,84},{24,88},{28,92},{32,9... | collective-permute-start | bytes 786440 | tf_op jit(solution)/shard_map/ppermute | solution.py:336
  47.5 34.9 %copy-start.1 = (f32[1024,384]{1,0:T(8,128)S(1)}, f32[1024,384]{1,0:T(8,128)}, u32[]{:S(2)}) copy-start(f32[1024,384]{1,0:T(8,128)} %get-tuple-element.33.lse_ref) | copy-start | bytes 4718596
  47.5 34.9 %copy-start.2 = (bf16[1024,384]{1,0:T(8,128)(2,1)S(1)}, bf16[1024,384]{1,0:T(8,128)(2,1)}, u32[]{:S(2)}) copy-start(bf16[1024,384]{1,0:T(8,128)(2,1)} %get-tuple-element.32.out_ref) | copy-start | bytes 2359300
  47.5 35.0 %copy-start.3 = (f32[1024,128]{1,0:T(8,128)S(1)}, f32[1024,128]{1,0:T(8,128)}, u32[]{:S(2)}) copy-start(f32[1024,128]{1,0:T(8,128)} %get-tuple-element.40.lse2_ref) | copy-start | bytes 1572868
  47.5 35.0 %copy-start.7 = (s32[8,2]{1,0:T(8,128)S(1)}, s32[8,2]{1,0:T(8,128)}, u32[]{:S(2)}) copy-start(s32[8,2]{1,0:T(8,128)} %copy.10.offsets_ref) | copy-start | bytes 196
  53.0 50.0 %collective-permute-start.10 = (bf16[256,2048]{1,0:T(8,128)(2,1)}, bf16[256,2048]{1,0:T(8,128)(2,1)}, u32[]{:S(2)}, u32[]{:S(2)}) collective-permute-start(bf16[256,2048]{1,0:T(8,128)(2,1)} %collective-permute-done.5.refs_2_), channel_id=1, source_target_pairs={{0,1},{1,0},{2,3},{3,2},{4,5},{5,4},{6,7},{7,6},{8,9},{9,8},{10,11... | collective-permute-start | bytes 3145736 | tf_op jit(solution)/shard_map/ppermute | solution.py:336
  55.6 47.4 %collective-permute-start.11 = (bf16[256,2048]{1,0:T(8,128)(2,1)}, bf16[256,2048]{1,0:T(8,128)(2,1)}, u32[]{:S(2)}, u32[]{:S(2)}) collective-permute-start(bf16[256,2048]{1,0:T(8,128)(2,1)} %collective-permute-done.6.refs_4_), channel_id=1, source_target_pairs={{0,1},{1,0},{2,3},{3,2},{4,5},{5,4},{6,7},{7,6},{8,9},{9,8},{10,11... | collective-permute-start | bytes 3145736 | tf_op jit(solution)/shard_map/ppermute | solution.py:336
  59.8 22.7 %copy-start.6 = (bf16[1024,128]{1,0:T(8,128)(2,1)S(1)}, bf16[1024,128]{1,0:T(8,128)(2,1)}, u32[]{:S(2)}) copy-start(bf16[1024,128]{1,0:T(8,128)(2,1)} %get-tuple-element.39.out2_ref) | copy-start | bytes 786436
  60.6 20.0 %all-to-all-start.1 = ((bf16[8,192,128]{2,1,0:T(8,128)(2,1)}), bf16[8,192,128]{2,1,0:T(8,128)(2,1)}, u32[]{:S(2)}, u32[]{:S(2)}) async-start(bf16[8,192,128]{2,1,0:T(8,128)(2,1)} %pad_maximum_fusion), calls=%async_computation.1 | async-start | bytes 786432 | tf_op jit(solution)/shard_map/all_to_all | solution.py:370
  87.1 5.5 %copy-start.5 = (bf16[512,2048]{1,0:T(8,128)(2,1)S(1)}, bf16[512,2048]{1,0:T(8,128)(2,1)}, u32[]{:S(2)}) copy-start(bf16[512,2048]{1,0:T(8,128)(2,1)} %refs_1_.1) | copy-start | bytes 6291460
  87.1 5.5 %collective-permute-start.7 = (bf16[256,512]{1,0:T(8,128)(2,1)S(1)}, bf16[256,512]{1,0:T(8,128)(2,1)S(1)}, u32[]{:S(2)}, u32[]{:S(2)}) collective-permute-start(bf16[256,512]{1,0:T(8,128)(2,1)S(1)} %combine_patterns.7), channel_id=1, source_target_pairs={{0,1},{1,0},{2,3},{3,2},{4,5},{5,4},{6,7},{7,6},{8,9},{9,8},{10,11... | collective-permute-start | bytes 786440 | tf_op jit(solution)/shard_map/ppermute | solution.py:336
  89.6 8.6 %collective-permute-start.9 = (bf16[256,512]{1,0:T(8,128)(2,1)S(1)}, bf16[256,512]{1,0:T(8,128)(2,1)S(1)}, u32[]{:S(2)}, u32[]{:S(2)}) collective-permute-start(bf16[256,512]{1,0:T(8,128)(2,1)S(1)} %combine_patterns.4), channel_id=1, source_target_pairs={{0,3},{1,2},{2,1},{3,0},{4,7},{5,6},{6,5},{7,4},{8,11},{9,10},{10,... | collective-permute-start | bytes 786440 | tf_op jit(solution)/shard_map/ppermute | solution.py:336
  90.2 12.8 %collective-permute-start.8 = (bf16[256,512]{1,0:T(8,128)(2,1)S(1)}, bf16[256,512]{1,0:T(8,128)(2,1)S(1)}, u32[]{:S(2)}, u32[]{:S(2)}) collective-permute-start(bf16[256,512]{1,0:T(8,128)(2,1)S(1)} %combine_patterns.5), channel_id=1, source_target_pairs={{0,2},{1,3},{2,0},{3,1},{4,6},{5,7},{6,4},{7,5},{8,10},{9,11},{10,... | collective-permute-start | bytes 786440 | tf_op jit(solution)/shard_map/ppermute | solution.py:336

commit v3 on v1

v3 whole, which is shorter than its diff:
```python
import functools

import jax
import jax.numpy as jnp
from jax import lax
from jax.experimental import pallas as pl
from jax.experimental.pallas import tpu as pltpu
from jax.sharding import PartitionSpec as P

HEAD_DIM = 64
NEAR_DILATION = 8
FAR_DILATION = 16
SEGMENT = 8
ROWS = 1024
NEAR_ROWS = ROWS // NEAR_DILATION
FAR_ROWS = ROWS // FAR_DILATION
QUARTER = ROWS // 4
NEAR_PART = QUARTER // NEAR_DILATION
FAR_PART = QUARTER // FAR_DILATION
QUARTER_PICKED = NEAR_PART + FAR_PART
PICKED = NEAR_ROWS + FAR_ROWS
SENT_ROWS = PICKED + PICKED // 2
PAIR = 2 * HEAD_DIM
NEG = -1e30
SCALE = HEAD_DIM ** -0.5
BF16 = jnp.bfloat16
F32 = jnp.float32
ROW_BLOCK = 128
VMEM_BYTES = 56 * 1024 * 1024
LESS_VMEM_BYTES = 20 * 1024 * 1024
SMALL = pl.CostEstimate(flops=1000, bytes_accessed=1000, transcendentals=0)


def lanes(shape):
    return lax.broadcasted_iota(jnp.int32, shape, 1)


def head_offsets(offsets_ref, head):
    near = lax.rem(offsets_ref[0, head], NEAR_DILATION)
    return near, lax.rem(offsets_ref[1, head], FAR_DILATION)


def one_hot(offset_near, offset_far):
    row = lax.broadcasted_iota(jnp.int32, (QUARTER_PICKED, QUARTER), 0)
    col = lax.broadcasted_iota(jnp.int32, (QUARTER_PICKED, QUARTER), 1)
    count = QUARTER // NEAR_DILATION
    at = jnp.where(
        row < count,
        row * NEAR_DILATION + offset_near,
        (row - count) * FAR_DILATION + offset_far,
    )
    return jnp.where(col == at, 1.0, 0.0).astype(BF16)


def pick_kernel(offsets_ref, q_ref, k_ref, v_ref, out_ref):
    heads = 2 * pl.num_programs(0)
    first = lax.axis_index("tp") * heads + 2 * pl.program_id(0)
    chosen = jnp.concatenate([one_hot(*head_offsets(offsets_ref, first + i)) for i in range(2)], 0)
    split = QUARTER // NEAR_DILATION
    found = []
    for i in range(ROWS // QUARTER):
        block = slice(i * QUARTER, (i + 1) * QUARTER)
        fields = jnp.concatenate([q_ref[block, :], k_ref[block, :], v_ref[block, :]], 1)
        found.append(jnp.dot(chosen, fields, preferred_element_type=F32))
    low = lanes((PICKED, PAIR)) < HEAD_DIM
    for side in range(2):
        base = side * QUARTER_PICKED
        part = jnp.concatenate(
            [f[base : base + split] for f in found]
            + [f[base + split : base + QUARTER_PICKED] for f in found],
            0,
        )
        q, k, v = (part[:, i * PAIR : (i + 1) * PAIR] for i in range(3))
        if side == 0:
            kv = jnp.where(low, k, pltpu.roll(v, HEAD_DIM, 1))
        else:
            kv = jnp.where(low, pltpu.roll(k, HEAD_DIM, 1), v)
        other = pltpu.roll(q, HEAD_DIM, 1)
        q_low, q_high = (q, other) if side == 0 else (other, q)
        q_packed = []
        for start, count in ((0, NEAR_ROWS), (NEAR_ROWS, FAR_ROWS)):
            half = count // 2
            q_packed.append(
                jnp.where(
                    lanes((half, PAIR)) < HEAD_DIM,
                    q_low[start : start + half],
                    q_high[start + half : start + count],
                )
            )
        out_ref[side, 0:PICKED, :] = kv.astype(BF16)
        out_ref[side, PICKED:SENT_ROWS, :] = (jnp.concatenate(q_packed, 0) * SCALE).astype(BF16)


def pick(queries, keys, values, offsets):
    heads = queries.shape[1] // HEAD_DIM
    pair_spec = pl.BlockSpec((ROWS, PAIR), lambda i: (0, i))
    return pl.pallas_call(
        pick_kernel,
        grid=(heads // 2,),
        in_specs=[pl.BlockSpec(memory_space=pltpu.SMEM)] + [pair_spec] * 3,
        out_specs=pl.BlockSpec((2, SENT_ROWS, PAIR), lambda i: (i, 0, 0)),
        out_shape=jax.ShapeDtypeStruct((heads, SENT_ROWS, PAIR), BF16),
        compiler_params=pltpu.CompilerParams(vmem_limit_bytes=VMEM_BYTES),
        cost_estimate=SMALL,
        name="pick_rows",
    )(offsets, queries, keys, values)


def contract_lanes(a, b):
    return lax.dot_general(a, b, (((1,), (1,)), ((), ())), preferred_element_type=F32)


def with_ones(v):
    return jnp.concatenate([v, jnp.ones_like(v)], 1)


def softmax_sum(scores, values):
    peak = functools.reduce(jnp.maximum, [jnp.max(s, axis=1, keepdims=True) for s in scores])
    acc = None
    for s, v in zip(scores, values):
        part = jnp.dot(jnp.exp(s - peak).astype(BF16), v, preferred_element_type=F32)
        acc = part if acc is None else acc + part
    total = acc[:, PAIR:]
    return acc[:, :PAIR] / total, peak + jnp.log(total)


def local_kernel(q_ref, k_ref, v_ref, pack_ref):
    pair = pl.program_id(0)
    keys = k_ref[...]
    values = with_ones(v_ref[...])
    low = lanes((ROW_BLOCK, PAIR)) < HEAD_DIM
    lane = lanes((ROW_BLOCK, PAIR))
    zero = jnp.zeros((), BF16)
    columns = pl.ds(pl.multiple_of(pair * PAIR, PAIR), PAIR)
    stats_at = pack_ref.shape[1] - PAIR
    for i in range(ROWS // ROW_BLOCK):
        rows = pl.ds(i * ROW_BLOCK, ROW_BLOCK)
        q = q_ref[rows, :] * jnp.asarray(SCALE, BF16)
        both = [
            softmax_sum([contract_lanes(jnp.where(mine, q, zero), keys)], [values])
            for mine in (low, jnp.logical_not(low))
        ]
        pack_ref[rows, columns] = jnp.where(low, both[0][0], both[1][0]).astype(BF16)
        lse = jnp.where((lane & 1) == 0, both[0][1], both[1][1])
        high = lse.astype(BF16)
        rest = (lse - high.astype(F32)).astype(BF16)
        stats = jnp.where(low, high.astype(F32), rest.astype(F32))
        held = pack_ref[rows, stats_at:].astype(F32)
        mine = (lane & (HEAD_DIM - 1)) // 2 == pair
        pack_ref[rows, stats_at:] = jnp.where(
            mine, stats, jnp.where(pair == 0, 0.0, held)
        ).astype(BF16)


def local_attention(queries, keys, values):
    spec = pl.BlockSpec((ROWS, PAIR), lambda i: (0, i))
    width = queries.shape[1] + PAIR
    return pl.pallas_call(
        local_kernel,
        grid=(queries.shape[1] // PAIR,),
        in_specs=[spec] * 3,
        out_specs=pl.BlockSpec((ROWS, width), lambda i: (0, 0)),
        out_shape=jax.ShapeDtypeStruct((ROWS, width), BF16),
        compiler_params=pltpu.CompilerParams(vmem_limit_bytes=VMEM_BYTES),
        cost_estimate=SMALL,
        name="local_attention",
    )(queries, keys, values)


def unpack_queries(packed):
    low = lanes(packed.shape) < HEAD_DIM
    wide = packed.astype(F32)
    top = jnp.where(low, wide, 0.0).astype(BF16)
    bottom = jnp.where(low, pltpu.roll(wide, HEAD_DIM, 1), 0.0).astype(BF16)
    return top, bottom


def result_rows(out, lse):
    high = lse.astype(BF16)
    rest = (lse - high.astype(F32)).astype(BF16)
    lane = lanes(out.shape)
    moved = pltpu.roll(out, HEAD_DIM, 1)
    stats = jnp.where(lane < HEAD_DIM + HEAD_DIM // 2, high.astype(F32), rest.astype(F32))
    return jnp.where(lane < HEAD_DIM, moved, stats).astype(BF16)


def near_kernel(sent_ref, out_ref):
    near_kv = jnp.concatenate([sent_ref[i, 0:NEAR_ROWS, :] for i in range(SEGMENT)], 0)
    near_values = with_ones(near_kv)
    half = NEAR_ROWS // 2
    for i in range(SEGMENT):
        q = jnp.concatenate(unpack_queries(sent_ref[i, PICKED : PICKED + half, :]), 0)
        res = result_rows(*softmax_sum([contract_lanes(q, near_kv)], [near_values]))
        for t in range(4):
            out_ref[t * SEGMENT + i] = res[t * NEAR_PART : (t + 1) * NEAR_PART]


def far_queries(sent_ref, i):
    half = FAR_ROWS // 2
    packed = jnp.concatenate(
        [sent_ref[2 * i + j, SENT_ROWS - half : SENT_ROWS, :] for j in range(2)], 0
    )
    return jnp.concatenate(unpack_queries(packed), 0)


def first_far_kernel(sent_ref, far0_ref, far1_ref, far2_ref, far3_ref, out_ref, lse_ref):
    far = [r[...] for r in (far0_ref, far1_ref, far2_ref, far3_ref)]
    far_values = [with_ones(f) for f in far]
    for i in range(SEGMENT // 2):
        q = far_queries(sent_ref, i)
        out, lse = softmax_sum([contract_lanes(q, f) for f in far], far_values)
        rows = slice(i * PAIR, (i + 1) * PAIR)
        out_ref[rows, :] = out
        lse_ref[rows, :] = lse


def second_far_kernel(
    sent_ref, near_ref, held_ref, held_lse_ref, far0_ref, far1_ref, far2_ref, far3_ref, out_ref
):
    far = [r[...] for r in (far0_ref, far1_ref, far2_ref, far3_ref)]
    far_values = [with_ones(f) for f in far]
    half = FAR_ROWS // 2
    out_ref[:, 0:NEAR_PART, :] = near_ref[...]
    for i in range(SEGMENT // 2):
        q = far_queries(sent_ref, i)
        out, lse = softmax_sum([contract_lanes(q, f) for f in far], far_values)
        rows = slice(i * PAIR, (i + 1) * PAIR)
        held, held_lse = held_ref[rows, :], held_lse_ref[rows, :]
        peak = jnp.maximum(lse, held_lse)
        new, old = jnp.exp(lse - peak), jnp.exp(held_lse - peak)
        both = new + old
        res = result_rows((new * out + old * held) / both, peak + jnp.log(both))
        for t in range(4):
            for j in range(2):
                at = ((t // 2) * 2 + j) * half + (t % 2) * FAR_PART
                out_ref[t * SEGMENT + 2 * i + j, NEAR_PART:, :] = res[at : at + FAR_PART]


def near_attention(sent):
    return pl.pallas_call(
        near_kernel,
        in_specs=[pl.BlockSpec(memory_space=pltpu.VMEM)],
        out_specs=pl.BlockSpec(memory_space=pltpu.VMEM),
        out_shape=jax.ShapeDtypeStruct((4 * SEGMENT, NEAR_PART, PAIR), BF16),
        compiler_params=pltpu.CompilerParams(vmem_limit_bytes=LESS_VMEM_BYTES),
        cost_estimate=SMALL,
        name="near_attention",
    )(sent)


def first_far_attention(sent, far):
    return pl.pallas_call(
        first_far_kernel,
        in_specs=[pl.BlockSpec(memory_space=pltpu.VMEM)] * 5,
        out_specs=[pl.BlockSpec(memory_space=pltpu.VMEM)] * 2,
        out_shape=[jax.ShapeDtypeStruct((SEGMENT * FAR_ROWS, PAIR), F32)] * 2,
        compiler_params=pltpu.CompilerParams(vmem_limit_bytes=LESS_VMEM_BYTES),
        cost_estimate=SMALL,
        name="first_far_attention",
    )(sent, *far)


def second_far_attention(sent, near_back, held, far):
    return pl.pallas_call(
        second_far_kernel,
        in_specs=[pl.BlockSpec(memory_space=pltpu.VMEM)] * 8,
        out_specs=pl.BlockSpec(memory_space=pltpu.VMEM),
        out_shape=jax.ShapeDtypeStruct((4 * SEGMENT, QUARTER_PICKED, PAIR), BF16),
        compiler_params=pltpu.CompilerParams(vmem_limit_bytes=LESS_VMEM_BYTES),
        cost_estimate=SMALL,
        name="second_far_attention",
    )(sent, near_back, *held, *far)


def combine_pair(offsets_ref, back_ref, head, out, lse, low_rows, position):
    outs, lses = [out], [lse]
    offsets = [head_offsets(offsets_ref, head + side) for side in range(2)]
    for which, (start, count, dilation) in enumerate(
        ((0, NEAR_PART, NEAR_DILATION), (NEAR_PART, FAR_PART, FAR_DILATION))
    ):
        offset = [o[which] for o in offsets]
        row = lax.broadcasted_iota(jnp.int32, (QUARTER, 2 * count), 0)
        col = lax.broadcasted_iota(jnp.int32, (QUARTER, 2 * count), 1)
        at = jnp.where(
            col < count, col * dilation + offset[0], (col - count) * dilation + offset[1]
        )
        placed = jnp.where(row == at, 1.0, 0.0).astype(BF16)
        low = lanes((count, PAIR)) < HEAD_DIM
        first = back_ref[head, start : start + count, :].astype(F32)
        second = back_ref[head + 1, start : start + count, :].astype(F32)
        zero = jnp.zeros((count, PAIR), F32)
        top = jnp.concatenate(
            [
                jnp.where(low, first, zero),
                jnp.where(low, first[:, 64:65], zero),
                jnp.where(low, first[:, 96:97], zero),
            ],
            1,
        )
        bottom = jnp.concatenate(
            [
                jnp.where(low, zero, pltpu.roll(second, HEAD_DIM, 1)),
                jnp.where(low, zero, second[:, 64:65]),
                jnp.where(low, zero, second[:, 96:97]),
            ],
            1,
        )
        wide = jnp.dot(
            placed, jnp.concatenate([top, bottom], 0).astype(BF16), preferred_element_type=F32
        )
        here = jnp.where(low_rows, offset[0], offset[1])
        hit = (position & (dilation - 1)) == here
        outs.append(wide[:, :PAIR])
        lses.append(jnp.where(hit, wide[:, PAIR : 2 * PAIR] + wide[:, 2 * PAIR :], NEG))
    peak = jnp.maximum(jnp.maximum(lses[0], lses[1]), lses[2])
    numer, denom = 0.0, 0.0
    for out, lse in zip(outs, lses):
        weight = jnp.exp(lse - peak)
        numer = numer + weight * out
        denom = denom + weight
    return (numer / denom).astype(BF16)


def finish_kernel(offsets_ref, pack_ref, back_ref, *refs):
    weight_refs, (total_ref, last_ref, held, sems) = refs[:-4], refs[-4:]
    depth = held.shape[1]
    copies = [
        pltpu.make_async_copy(weight, held.at[i], sems.at[i]) for i, weight in enumerate(weight_refs)
    ]
    for copy in copies:
        copy.start()
    place = lax.axis_index("tp")
    heads = depth // HEAD_DIM
    low_rows = lanes((QUARTER, PAIR)) < HEAD_DIM
    position = lax.broadcasted_iota(jnp.int32, (QUARTER, PAIR), 0)
    source = lax.broadcasted_iota(jnp.int32, (PAIR, depth), 0) & (HEAD_DIM - 1)
    widen = jnp.where(source == lanes((PAIR, depth)) // HEAD_DIM, 1.0, 0.0).astype(BF16)
    for i in range(4):
        who = place ^ i
        rows = pl.ds(pl.multiple_of(who * QUARTER, QUARTER), QUARTER)
        lse = jnp.dot(pack_ref[rows, depth:], widen, preferred_element_type=F32)
        attn = []
        for pair in range(depth // PAIR):
            columns = slice(pair * PAIR, (pair + 1) * PAIR)
            attn.append(
                combine_pair(
                    offsets_ref,
                    back_ref,
                    who * heads + 2 * pair,
                    pack_ref[rows, columns].astype(F32),
                    lse[:, columns],
                    low_rows,
                    position,
                )
            )
        attn = jnp.concatenate(attn, 1)
        if i == 3:
            last_ref[...] = attn
            continue
        copies[i].wait()
        for start in range(0, total_ref.shape[1], 512):
            columns = slice(start, start + 512)
            part = jnp.dot(attn, held[i, :, columns], preferred_element_type=F32)
            if i > 0:
                part = part + total_ref[:, columns]
            total_ref[:, columns] = part


def finish(offsets, pack, back, weights):
    depth, width = weights[0].shape
    vmem = pl.BlockSpec(memory_space=pltpu.VMEM)
    return pl.pallas_call(
        finish_kernel,
        in_specs=[pl.BlockSpec(memory_space=pltpu.SMEM), vmem, vmem]
        + [pl.BlockSpec(memory_space=pl.ANY)] * len(weights),
        out_specs=[vmem, vmem],
        out_shape=[
            jax.ShapeDtypeStruct((QUARTER, width), F32),
            jax.ShapeDtypeStruct((QUARTER, depth), BF16),
        ],
        scratch_shapes=[
            pltpu.VMEM((len(weights), depth, width), BF16),
            pltpu.SemaphoreType.DMA((len(weights),)),
        ],
        compiler_params=pltpu.CompilerParams(vmem_limit_bytes=40 * 1024 * 1024),
        cost_estimate=SMALL,
        name="finish",
    )(offsets, pack, back, *weights)


def last_kernel(total_ref, rows_ref, weight_ref, out_ref):
    part = jnp.dot(rows_ref[...], weight_ref[...], preferred_element_type=F32)
    out_ref[...] = (total_ref[...] + part).astype(BF16)


def add_last(total, rows, weight):
    width = 512
    column = lambda i: (0, i)
    return pl.pallas_call(
        last_kernel,
        grid=(total.shape[1] // width,),
        in_specs=[
            pl.BlockSpec((QUARTER, width), column),
            pl.BlockSpec(rows.shape, lambda i: (0, 0)),
            pl.BlockSpec((weight.shape[0], width), column),
        ],
        out_specs=pl.BlockSpec((QUARTER, width), column),
        out_shape=jax.ShapeDtypeStruct(total.shape, BF16),
        compiler_params=pltpu.CompilerParams(vmem_limit_bytes=LESS_VMEM_BYTES),
        cost_estimate=SMALL,
        name="add_last",
    )(total, rows, weight)


def swap(shard, axis, bits):
    return lax.ppermute(shard, axis, [(i, i ^ bits) for i in range(lax.axis_size(axis))])


def local(queries, keys, values, offsets, out_weight):
    n_tp, n_ctx = lax.axis_size("tp"), lax.axis_size("ctx")
    offsets = offsets.T
    segments = [[s * SEGMENT + i for i in range(SEGMENT)] for s in range(n_ctx // SEGMENT)]
    owners = [[c * n_tp + t for t in range(n_tp) for c in segment] for segment in segments]
    across = [(c * n_tp + t, (c ^ (t & 1)) * n_tp + (t ^ 2)) for c in range(n_ctx) for t in range(n_tp)]

    picked = pick(queries, keys, values, offsets)
    picked, sent_weight = lax.optimization_barrier((picked, out_weight))
    sent = lax.all_to_all(picked, "ctx", 0, 0, axis_index_groups=segments, tiled=True)
    weight_2 = lax.ppermute(sent_weight, ("ctx", "tp"), across)
    pack = local_attention(queries, keys, values)
    sent, pack = lax.optimization_barrier((sent, pack))

    first = sent[:, NEAR_ROWS:PICKED, :].reshape(SEGMENT * FAR_ROWS, PAIR)
    second = swap(first, "ctx", 8)
    first = [first] + [swap(first, "ctx", 16 * i) for i in (1, 2, 3)]
    pack = lax.all_to_all(pack, "tp", 0, 0, tiled=True)
    second, near_sent = lax.optimization_barrier((second, sent))
    near_back = near_attention(near_sent)
    second = [second] + [swap(second, "ctx", 16 * i) for i in (1, 2, 3)]
    held = first_far_attention(sent, first)
    held, near_back, sent_weight = lax.optimization_barrier((held, near_back, out_weight))
    weight_1 = swap(sent_weight, "tp", 1)
    held, second = lax.optimization_barrier((held, second))
    back = second_far_attention(sent, near_back, held, second)
    back, pack = lax.optimization_barrier((back, pack))
    back = lax.all_to_all(back, ("ctx", "tp"), 0, 0, axis_index_groups=owners, tiled=True)
    back, weight_2 = lax.optimization_barrier((back, weight_2))
    weight_3 = swap(weight_2, "tp", 1)
    total, rows = finish(offsets, pack, back, [out_weight, weight_1, weight_2])
    return add_last(total, rows, weight_3)


def solution(mesh):
    return jax.shard_map(
        local,
        mesh=mesh,
        in_specs=(P("ctx", "tp"), P("ctx", "tp"), P("ctx", "tp"), P(), P("tp", None)),
        out_specs=P(("ctx", "tp"), None),
        check_vma=False,
    )
```

time: 128 us -> 91.2 us (0.71)
  blocking collectives: 26.1 us -> 0 us
  starting transfers between devices: 20.7 us -> 39.6 us
  local copies, waits for them, and re-layouts: 12.9 us -> 0.02 us
  Pallas kernels: 39.6 us -> 33.9 us
  matrix products: 4.18 us -> 0 us
  waiting for transfers between devices: 20.3 us -> 17.1 us
  other arithmetic: 2.92 us -> 0 us
    all_to_all x1 -> x0, blocking collectives: 26.1 us -> none  [local(): lax.all_to_all(picked, 'ctx', 0, 0, axis_index_groups=segments, tiled=True)]
    ppermute x7 -> x9, waiting for transfers between devices: 20.3 us -> 3.31 us  [swap(): lax.ppermute(shard, axis, [(i, i ^ bits) for i in range(lax.axis_size(axi...]
    all_to_all x1 -> x3, starting transfers between devices: 7.39 us -> 22.3 us  [the longest x1 9.35 us: local(): lax.all_to_all(back, ('ctx', 'tp'), 0, 0, axis_index_groups=owners, tiled...]
    all_to_all x1 -> x3, waiting for transfers between devices: 0.01 us -> 13.8 us  [the longest x1 13.8 us: local(): lax.all_to_all(back, ('ctx', 'tp'), 0, 0, axis_index_groups=owners, tiled...]
    unnamed x24 -> x2, local copies, waits for them, and re-layouts: 10.9 us -> 0.01 us
    pallas_call x3 -> x6, Pallas kernels: 35.4 us -> 29.6 us  [the longest x1 13.7 us: local_attention(): pl.pallas_call(local_kernel, grid=(queries.shape[1] // PAIR,), in_specs=[...]
    dot_general x2 -> x0, matrix products: 4.18 us -> none  [the longest x1 2.83 us: local(): jnp.dot(came, weight_there, preferred_element_type=F32)]
    convert_element_type x1 -> x0, other arithmetic: 2.88 us -> none  [local(): return (keep + swap(give, 'tp', 1).astype(F32)).astype(BF16)]
  transfers between devices with their start and end apart: 9 -> 13, of which waited for: 6 -> 4; matrix products, arithmetic and copies ran while one was open for 1% -> 0% of each run, Pallas kernels for 28% -> 30%
where the time goes in v3:
time: 91.2 us; the launch traced here: 90.8 us
  starting transfers between devices  39.6 us (43%)
  Pallas kernels  33.9 us (37%)
  waiting for transfers between devices  17.1 us (19%)
    ppermute x9, starting transfers between devices, swap(): lax.ppermute(shard, axis, [(i, i ^ bits) for i in range(lax.axis_size(axi...  14.5 us
    all_to_all x1, waiting for transfers between devices, local(): lax.all_to_all(back, ('ctx', 'tp'), 0, 0, axis_index_groups=owners, tiled...  13.8 us
    pallas_call x1, Pallas kernels, local_attention(): pl.pallas_call(local_kernel, grid=(queries.shape[1] // PAIR,), in_specs=[...  13.7 us
    all_to_all x1, starting transfers between devices, local(): lax.all_to_all(back, ('ctx', 'tp'), 0, 0, axis_index_groups=owners, tiled...  9.35 us
    all_to_all x1, starting transfers between devices, local(): lax.all_to_all(picked, 'ctx', 0, 0, axis_index_groups=segments, tiled=True)  9.08 us
    pallas_call x1, Pallas kernels, finish(): pl.pallas_call(finish_kernel, in_specs=[pl.BlockSpec(memory_space=pltpu.S...  7.08 us
    pallas_call x1, Pallas kernels, pick(): pl.pallas_call(pick_kernel, grid=(heads // 2,), in_specs=[pl.BlockSpec(me...  4.32 us
    all_to_all x1, starting transfers between devices, local(): pack = lax.all_to_all(pack, 'tp', 0, 0, tiled=True)  3.91 us
  transfers between devices with their start and end apart: 13, of which 4 were waited for; matrix products, arithmetic and copies ran while one was open for 0% of the time, Pallas kernels for 30%

profile of v3, /device:TPU:1, one launch (start us, length us, event | category | flops | bytes accessed | tf_op | source)
XLA Modules:
  0.0 90.8 jit_solution(12074719997702003216)
XLA Ops:
  0.0 4.3 %pick_rows.1 = bf16[8,288,128]{2,1,0:T(8,128)(2,1)} custom-call(s32[2,32]{1,0:T(2,128)} %bitcast.10, bf16[1024,512]{1,0:T(8,128)(2,1)} %q_ref.3, bf16[1024,512]{1,0:T(8,128)(2,1)} %k_ref.3, bf16[1024,512]{1,0:T(8,128)(2,1)} %v_ref.3), custom_call_target="tpu_custom_call" | custom-call | flops 1000 | bytes 1000 | tf_op jit(solution)/shard_map/pick_rows/pallas_call | solution.py:97
  4.3 9.1 %all-to-all-start = ((bf16[8,288,128]{2,1,0:T(8,128)(2,1)}), bf16[8,288,128]{2,1,0:T(8,128)(2,1)S(1)}, u32[]{:S(2)}, u32[]{:S(2)}) async-start(bf16[8,288,128]{2,1,0:T(8,128)(2,1)} %pick_rows.1), calls=%async_computation | async-start | bytes 1179648 | tf_op jit(solution)/shard_map/all_to_all | solution.py:428
  13.4 2.8 %collective-permute-start.7 = (bf16[512,2048]{1,0:T(8,128)(2,1)}, bf16[512,2048]{1,0:T(8,128)(2,1)}, u32[]{:S(2)}, u32[]{:S(2)}) collective-permute-start(bf16[512,2048]{1,0:T(8,128)(2,1)} %refs_0_.1), channel_id=1, source_target_pairs={{0,2},{1,7},{2,0},{3,5},{4,6},{5,3},{6,4},{7,1},{8,10},{9,15},{10,... | collective-permute-start | bytes 6291464 | tf_op jit(solution)/shard_map/ppermute | solution.py:429
  16.2 13.7 %local_attention.1 = bf16[1024,640]{1,0:T(8,128)(2,1)} custom-call(bf16[1024,512]{1,0:T(8,128)(2,1)} %q_ref.3, bf16[1024,512]{1,0:T(8,128)(2,1)} %k_ref.3, bf16[1024,512]{1,0:T(8,128)(2,1)} %v_ref.3), custom_call_target="tpu_custom_call" | custom-call | flops 1000 | bytes 1000 | tf_op jit(solution)/shard_map/local_attention/pallas_call | solution.py:158
  29.8 0.0 all-to-all-done.sent_ref
  29.8 3.9 %all-to-all-start.1 = ((bf16[4,256,640]{2,1,0:T(8,128)(2,1)}), bf16[4,256,640]{2,1,0:T(8,128)(2,1)S(1)}, u32[]{:S(2)}, u32[]{:S(2)}) async-start(bf16[4,256,640]{2,1,0:T(8,128)(2,1)} %bitcast.12), calls=%async_computation.1 | async-start | bytes 2621440 | tf_op jit(solution)/shard_map/all_to_all | solution.py:436
  33.8 4.3 %collective-permute-start.3 = (bf16[512,128]{1,0:T(8,128)(2,1)S(1)}, bf16[512,128]{1,0:T(8,128)(2,1)S(1)}, u32[]{:S(2)}, u32[]{:S(2)}) collective-permute-start(bf16[512,128]{1,0:T(8,128)(2,1)S(1)} %bitcast.5), channel_id=1, source_target_pairs={{0,32},{4,36},{8,40},{12,44},{16,48},{20,52},{24,56},{28,60},{32,0... | collective-permute-start | bytes 393224 | tf_op jit(solution)/shard_map/ppermute | solution.py:416
  38.1 2.5 %collective-permute-start.2 = (bf16[512,128]{1,0:T(8,128)(2,1)S(1)}, bf16[512,128]{1,0:T(8,128)(2,1)S(1)}, u32[]{:S(2)}, u32[]{:S(2)}) collective-permute-start(bf16[512,128]{1,0:T(8,128)(2,1)S(1)} %bitcast.6), channel_id=1, source_target_pairs={{0,192},{4,196},{8,200},{12,204},{16,208},{20,212},{24,216},{28,22... | collective-permute-start | bytes 393224 | tf_op jit(solution)/shard_map/ppermute | solution.py:416
  40.5 0.5 collective-permute-start.1
  41.1 0.3 collective-permute-start
  41.3 1.5 %collective-permute-done.3.far0_ref = bf16[512,128]{1,0:T(8,128)(2,1)S(1)} collective-permute-done((bf16[512,128]{1,0:T(8,128)(2,1)S(1)}, bf16[512,128]{1,0:T(8,128)(2,1)S(1)}, u32[]{:S(2)}, u32[]{:S(2)}) %collective-permute-start.3) | collective-permute-done | bytes 131104 | tf_op jit(solution)/shard_map/ppermute | solution.py:416
  42.8 2.5 %collective-permute-start.6 = (bf16[512,128]{1,0:T(8,128)(2,1)S(1)}, bf16[512,128]{1,0:T(8,128)(2,1)S(1)}, u32[]{:S(2)}, u32[]{:S(2)}) collective-permute-start(bf16[512,128]{1,0:T(8,128)(2,1)S(1)} %collective-permute-done.3.far0_ref), channel_id=1, source_target_pairs={{0,192},{4,196},{8,200},{12,204},{16,208},{20,212},{24,216},{28,22... | collective-permute-start | bytes 393224 | tf_op jit(solution)/shard_map/ppermute | solution.py:416
  45.3 0.6 collective-permute-done.2.far3_ref
  46.0 1.7 %collective-permute-start.5 = (bf16[512,128]{1,0:T(8,128)(2,1)S(1)}, bf16[512,128]{1,0:T(8,128)(2,1)S(1)}, u32[]{:S(2)}, u32[]{:S(2)}) collective-permute-start(bf16[512,128]{1,0:T(8,128)(2,1)S(1)} %collective-permute-done.3.far0_ref), channel_id=1, source_target_pairs={{0,128},{4,132},{8,136},{12,140},{16,144},{20,148},{24,152},{28,15... | collective-permute-start | bytes 393224 | tf_op jit(solution)/shard_map/ppermute | solution.py:416
  47.7 0.0 collective-permute-done.1.far2_ref
  47.7 2.4 %collective-permute-start.4 = (bf16[512,128]{1,0:T(8,128)(2,1)S(1)}, bf16[512,128]{1,0:T(8,128)(2,1)S(1)}, u32[]{:S(2)}, u32[]{:S(2)}) collective-permute-start(bf16[512,128]{1,0:T(8,128)(2,1)S(1)} %collective-permute-done.3.far0_ref), channel_id=1, source_target_pairs={{0,64},{4,68},{8,72},{12,76},{16,80},{20,84},{24,88},{28,92},{32,9... | collective-permute-start | bytes 393224 | tf_op jit(solution)/shard_map/ppermute | solution.py:416
  50.1 1.9 %near_attention.1.near_ref = bf16[32,32,128]{2,1,0:T(8,128)(2,1)S(1)} custom-call(bf16[8,288,128]{2,1,0:T(8,128)(2,1)S(1)} %all-to-all-done.sent_ref), custom_call_target="tpu_custom_call" | custom-call | flops 1000 | bytes 1000 | tf_op jit(solution)/shard_map/near_attention/pallas_call | solution.py:240
  52.0 0.0 copy-start
  52.0 0.0 collective-permute-done.far1_ref
  52.0 1.8 %first_far_attention.1 = (f32[512,128]{1,0:T(8,128)S(1)}, f32[512,128]{1,0:T(8,128)S(1)}) custom-call(bf16[8,288,128]{2,1,0:T(8,128)(2,1)S(1)} %all-to-all-done.sent_ref, bf16[512,128]{1,0:T(8,128)(2,1)S(1)} %bitcast.9, bf16[512,128]{1,0:T(8,128)(2,1)S(1)} %collective-permute-done.far1_ref, bf16[512,128]{1,0:T(8,128)(2,1)S(1)} %collective-permute-done.1.far2_ref, ...), custom_call_target="tpu_custom_call" | custom-call | flops 1000 | bytes 1000 | tf_op jit(solution)/shard_map/first_far_attention/pallas_call | solution.py:252
  53.8 0.0 collective-permute-done.6.far3_ref
  53.8 0.0 collective-permute-done.5.far2_ref
  53.8 1.1 %collective-permute-done.4.far1_ref = bf16[512,128]{1,0:T(8,128)(2,1)S(1)} collective-permute-done((bf16[512,128]{1,0:T(8,128)(2,1)S(1)}, bf16[512,128]{1,0:T(8,128)(2,1)S(1)}, u32[]{:S(2)}, u32[]{:S(2)}) %collective-permute-start.4) | collective-permute-done | bytes 131104 | tf_op jit(solution)/shard_map/ppermute | solution.py:416
  54.9 2.6 %second_far_attention.1 = bf16[32,48,128]{2,1,0:T(8,128)(2,1)} custom-call(bf16[8,288,128]{2,1,0:T(8,128)(2,1)S(1)} %all-to-all-done.sent_ref, bf16[32,32,128]{2,1,0:T(8,128)(2,1)S(1)} %near_attention.1.near_ref, f32[512,128]{1,0:T(8,128)S(1)} %get-tuple-element.38.held_ref, f32[512,128]{1,0:T(8,128)S(1)} %get-tuple-element.39.held_lse_ref, ...), custom_call_target="tpu_custom_call" | custom-call | flops 1000 | bytes 1000 | tf_op jit(solution)/shard_map/second_far_attention/pallas_call | solution.py:264
  57.6 0.0 all-to-all-done.1
  57.6 9.3 %all-to-all-start.2 = ((bf16[32,48,128]{2,1,0:T(8,128)(2,1)}), bf16[32,48,128]{2,1,0:T(8,128)(2,1)S(1)}, u32[]{:S(2)}, u32[]{:S(2)}) async-start(bf16[32,48,128]{2,1,0:T(8,128)(2,1)} %second_far_attention.1), calls=%async_computation.2 | async-start | bytes 786432 | tf_op jit(solution)/shard_map/all_to_all | solution.py:446
  66.9 0.3 collective-permute-start.8
  67.2 0.0 collective-permute-done.7.refs_2_
  67.3 13.8 %all-to-all-done.2.back_ref = bf16[32,48,128]{2,1,0:T(8,128)(2,1)S(1)} async-done(((bf16[32,48,128]{2,1,0:T(8,128)(2,1)}), bf16[32,48,128]{2,1,0:T(8,128)(2,1)S(1)}, u32[]{:S(2)}, u32[]{:S(2)}) %all-to-all-start.2) | async-done | bytes 393248 | tf_op jit(solution)/shard_map/all_to_all | solution.py:446
  81.1 0.0 collective-permute-start.9
  81.1 0.0 collective-permute-done.8.refs_1_
  81.1 0.0 copy-done
  81.1 7.1 %finish.1 = (f32[256,2048]{1,0:T(8,128)S(1)}, bf16[256,512]{1,0:T(8,128)(2,1)S(1)}) custom-call(s32[2,32]{1,0:T(2,128)S(1)} %bitcast.11, bf16[1024,640]{1,0:T(8,128)(2,1)S(1)} %bitcast.4, bf16[32,48,128]{2,1,0:T(8,128)(2,1)S(1)} %all-to-all-done.2.back_ref, bf16[512,2048]{1,0:T(8,128)(2,1)} %refs_0_.1, bf16[512,2048]{1,0:T(8,128)(2,1)} %collective-permute-done.8.refs_1_, ...), custom_call_target="tpu_custom_call" | custom-call | flops 1000 | bytes 1000 | tf_op jit(solution)/shard_map/finish/pallas_call | solution.py:372
  88.2 0.0 collective-permute-done.9.weight_ref
  88.2 2.6 %add_last.1 = bf16[256,2048]{1,0:T(8,128)(2,1)} custom-call(f32[256,2048]{1,0:T(8,128)S(1)} %get-tuple-element.51.total_ref, bf16[256,512]{1,0:T(8,128)(2,1)S(1)} %get-tuple-element.52.rows_ref, bf16[512,2048]{1,0:T(8,128)(2,1)S(1)} %collective-permute-done.9.weight_ref), custom_call_target="tpu_custom_call" | custom-call | flops 1000 | bytes 1000 | tf_op jit(solution)/shard_map/add_last/pallas_call | solution.py:399
  (1 shorter events, 0.0 us)
Async XLA Ops:
  4.3 25.5 %all-to-all-start = ((bf16[8,288,128]{2,1,0:T(8,128)(2,1)}), bf16[8,288,128]{2,1,0:T(8,128)(2,1)S(1)}, u32[]{:S(2)}, u32[]{:S(2)}) async-start(bf16[8,288,128]{2,1,0:T(8,128)(2,1)} %pick_rows.1), calls=%async_computation | async-start | bytes 1179648 | tf_op jit(solution)/shard_map/all_to_all | solution.py:428
  13.4 53.8 %collective-permute-start.7 = (bf16[512,2048]{1,0:T(8,128)(2,1)}, bf16[512,2048]{1,0:T(8,128)(2,1)}, u32[]{:S(2)}, u32[]{:S(2)}) collective-permute-start(bf16[512,2048]{1,0:T(8,128)(2,1)} %refs_0_.1), channel_id=1, source_target_pairs={{0,2},{1,7},{2,0},{3,5},{4,6},{5,3},{6,4},{7,1},{8,10},{9,15},{10,... | collective-permute-start | bytes 6291464 | tf_op jit(solution)/shard_map/ppermute | solution.py:429
  29.8 27.7 %all-to-all-start.1 = ((bf16[4,256,640]{2,1,0:T(8,128)(2,1)}), bf16[4,256,640]{2,1,0:T(8,128)(2,1)S(1)}, u32[]{:S(2)}, u32[]{:S(2)}) async-start(bf16[4,256,640]{2,1,0:T(8,128)(2,1)} %bitcast.12), calls=%async_computation.1 | async-start | bytes 2621440 | tf_op jit(solution)/shard_map/all_to_all | solution.py:436
  33.8 9.1 %collective-permute-start.3 = (bf16[512,128]{1,0:T(8,128)(2,1)S(1)}, bf16[512,128]{1,0:T(8,128)(2,1)S(1)}, u32[]{:S(2)}, u32[]{:S(2)}) collective-permute-start(bf16[512,128]{1,0:T(8,128)(2,1)S(1)} %bitcast.5), channel_id=1, source_target_pairs={{0,32},{4,36},{8,40},{12,44},{16,48},{20,52},{24,56},{28,60},{32,0... | collective-permute-start | bytes 393224 | tf_op jit(solution)/shard_map/ppermute | solution.py:416
  38.1 7.9 %collective-permute-start.2 = (bf16[512,128]{1,0:T(8,128)(2,1)S(1)}, bf16[512,128]{1,0:T(8,128)(2,1)S(1)}, u32[]{:S(2)}, u32[]{:S(2)}) collective-permute-start(bf16[512,128]{1,0:T(8,128)(2,1)S(1)} %bitcast.6), channel_id=1, source_target_pairs={{0,192},{4,196},{8,200},{12,204},{16,208},{20,212},{24,216},{28,22... | collective-permute-start | bytes 393224 | tf_op jit(solution)/shard_map/ppermute | solution.py:416
  40.5 7.2 %collective-permute-start.1 = (bf16[512,128]{1,0:T(8,128)(2,1)S(1)}, bf16[512,128]{1,0:T(8,128)(2,1)S(1)}, u32[]{:S(2)}, u32[]{:S(2)}) collective-permute-start(bf16[512,128]{1,0:T(8,128)(2,1)S(1)} %bitcast.7), channel_id=1, source_target_pairs={{0,128},{4,132},{8,136},{12,140},{16,144},{20,148},{24,152},{28,15... | collective-permute-start | bytes 393224 | tf_op jit(solution)/shard_map/ppermute | solution.py:416
  41.1 10.9 %collective-permute-start = (bf16[512,128]{1,0:T(8,128)(2,1)S(1)}, bf16[512,128]{1,0:T(8,128)(2,1)S(1)}, u32[]{:S(2)}, u32[]{:S(2)}) collective-permute-start(bf16[512,128]{1,0:T(8,128)(2,1)S(1)} %bitcast.8), channel_id=1, source_target_pairs={{0,64},{4,68},{8,72},{12,76},{16,80},{20,84},{24,88},{28,92},{32,9... | collective-permute-start | bytes 393224 | tf_op jit(solution)/shard_map/ppermute | solution.py:416
  42.8 10.9 %collective-permute-start.6 = (bf16[512,128]{1,0:T(8,128)(2,1)S(1)}, bf16[512,128]{1,0:T(8,128)(2,1)S(1)}, u32[]{:S(2)}, u32[]{:S(2)}) collective-permute-start(bf16[512,128]{1,0:T(8,128)(2,1)S(1)} %collective-permute-done.3.far0_ref), channel_id=1, source_target_pairs={{0,192},{4,196},{8,200},{12,204},{16,208},{20,212},{24,216},{28,22... | collective-permute-start | bytes 393224 | tf_op jit(solution)/shard_map/ppermute | solution.py:416
  46.0 7.8 %collective-permute-start.5 = (bf16[512,128]{1,0:T(8,128)(2,1)S(1)}, bf16[512,128]{1,0:T(8,128)(2,1)S(1)}, u32[]{:S(2)}, u32[]{:S(2)}) collective-permute-start(bf16[512,128]{1,0:T(8,128)(2,1)S(1)} %collective-permute-done.3.far0_ref), channel_id=1, source_target_pairs={{0,128},{4,132},{8,136},{12,140},{16,144},{20,148},{24,152},{28,15... | collective-permute-start | bytes 393224 | tf_op jit(solution)/shard_map/ppermute | solution.py:416
  47.7 7.2 %collective-permute-start.4 = (bf16[512,128]{1,0:T(8,128)(2,1)S(1)}, bf16[512,128]{1,0:T(8,128)(2,1)S(1)}, u32[]{:S(2)}, u32[]{:S(2)}) collective-permute-start(bf16[512,128]{1,0:T(8,128)(2,1)S(1)} %collective-permute-done.3.far0_ref), channel_id=1, source_target_pairs={{0,64},{4,68},{8,72},{12,76},{16,80},{20,84},{24,88},{28,92},{32,9... | collective-permute-start | bytes 393224 | tf_op jit(solution)/shard_map/ppermute | solution.py:416
  52.0 29.1 %copy-start = (s32[32,2]{0,1:T(2,128)S(1)}, s32[32,2]{0,1:T(2,128)}, u32[]{:S(2)}) copy-start(s32[32,2]{0,1:T(2,128)} %param.8) | copy-start | bytes 772
  57.6 23.5 %all-to-all-start.2 = ((bf16[32,48,128]{2,1,0:T(8,128)(2,1)}), bf16[32,48,128]{2,1,0:T(8,128)(2,1)S(1)}, u32[]{:S(2)}, u32[]{:S(2)}) async-start(bf16[32,48,128]{2,1,0:T(8,128)(2,1)} %second_far_attention.1), calls=%async_computation.2 | async-start | bytes 786432 | tf_op jit(solution)/shard_map/all_to_all | solution.py:446
  66.9 14.2 %collective-permute-start.8 = (bf16[512,2048]{1,0:T(8,128)(2,1)}, bf16[512,2048]{1,0:T(8,128)(2,1)}, u32[]{:S(2)}, u32[]{:S(2)}) collective-permute-start(bf16[512,2048]{1,0:T(8,128)(2,1)} %refs_0_.1), channel_id=1, source_target_pairs={{0,1},{1,0},{2,3},{3,2},{4,5},{5,4},{6,7},{7,6},{8,9},{9,8},{10,11... | collective-permute-start | bytes 6291464 | tf_op jit(solution)/shard_map/ppermute | solution.py:416
  81.1 7.1 %collective-permute-start.9 = (bf16[512,2048]{1,0:T(8,128)(2,1)}, bf16[512,2048]{1,0:T(8,128)(2,1)S(1)}, u32[]{:S(2)}, u32[]{:S(2)}) collective-permute-start(bf16[512,2048]{1,0:T(8,128)(2,1)} %collective-permute-done.7.refs_2_), channel_id=1, source_target_pairs={{0,1},{1,0},{2,3},{3,2},{4,5},{5,4},{6,7},{7,6},{8,9},{9,8},{10,11... | collective-permute-start | bytes 6291464 | tf_op jit(solution)/shard_map/ppermute | solution.py:416

commit v4 on v3

--- a/solution.py
+++ b/solution.py
@@ -279,39 +279,29 @@
         ((0, NEAR_PART, NEAR_DILATION), (NEAR_PART, FAR_PART, FAR_DILATION))
     ):
         offset = [o[which] for o in offsets]
-        row = lax.broadcasted_iota(jnp.int32, (QUARTER, 2 * count), 0)
-        col = lax.broadcasted_iota(jnp.int32, (QUARTER, 2 * count), 1)
-        at = jnp.where(
-            col < count, col * dilation + offset[0], (col - count) * dilation + offset[1]
-        )
+        row = lax.broadcasted_iota(jnp.int32, (QUARTER, 4 * count), 0)
+        col = lax.broadcasted_iota(jnp.int32, (QUARTER, 4 * count), 1)
+        at = (col & (count - 1)) * dilation + jnp.where((col & count) == 0, offset[0], offset[1])
         placed = jnp.where(row == at, 1.0, 0.0).astype(BF16)
         low = lanes((count, PAIR)) < HEAD_DIM
         first = back_ref[head, start : start + count, :].astype(F32)
         second = back_ref[head + 1, start : start + count, :].astype(F32)
         zero = jnp.zeros((count, PAIR), F32)
-        top = jnp.concatenate(
-            [
-                jnp.where(low, first, zero),
-                jnp.where(low, first[:, 64:65], zero),
-                jnp.where(low, first[:, 96:97], zero),
-            ],
-            1,
-        )
-        bottom = jnp.concatenate(
-            [
-                jnp.where(low, zero, pltpu.roll(second, HEAD_DIM, 1)),
-                jnp.where(low, zero, second[:, 64:65]),
-                jnp.where(low, zero, second[:, 96:97]),
-            ],
-            1,
-        )
+        moved = pltpu.roll(second, HEAD_DIM, 1)
+        content = [
+            (jnp.where(low, first, zero), jnp.where(low, first[:, 64:65], zero)),
+            (jnp.where(low, zero, moved), jnp.where(low, zero, second[:, 64:65])),
+            (zero, jnp.where(low, first[:, 96:97], zero)),
+            (zero, jnp.where(low, zero, second[:, 96:97])),
+        ]
+        content = jnp.concatenate([jnp.concatenate(part, 1) for part in content], 0)
         wide = jnp.dot(
-            placed, jnp.concatenate([top, bottom], 0).astype(BF16), preferred_element_type=F32
+            placed, content.astype(BF16), preferred_element_type=F32
         )
         here = jnp.where(low_rows, offset[0], offset[1])
         hit = (position & (dilation - 1)) == here
         outs.append(wide[:, :PAIR])
-        lses.append(jnp.where(hit, wide[:, PAIR : 2 * PAIR] + wide[:, 2 * PAIR :], NEG))
+        lses.append(jnp.where(hit, wide[:, PAIR:], NEG))
     peak = jnp.maximum(jnp.maximum(lses[0], lses[1]), lses[2])
     numer, denom = 0.0, 0.0
     for out, lse in zip(outs, lses):
@@ -389,22 +379,19 @@
 
 
 def last_kernel(total_ref, rows_ref, weight_ref, out_ref):
-    part = jnp.dot(rows_ref[...], weight_ref[...], preferred_element_type=F32)
-    out_ref[...] = (total_ref[...] + part).astype(BF16)
+    rows = rows_ref[...]
+    for start in range(0, out_ref.shape[1], 512):
+        columns = slice(start, start + 512)
+        part = jnp.dot(rows, weight_ref[:, columns], preferred_element_type=F32)
+        out_ref[:, columns] = (total_ref[:, columns] + part).astype(BF16)
 
 
 def add_last(total, rows, weight):
-    width = 512
-    column = lambda i: (0, i)
+    vmem = pl.BlockSpec(memory_space=pltpu.VMEM)
     return pl.pallas_call(
         last_kernel,
-        grid=(total.shape[1] // width,),
-        in_specs=[
-            pl.BlockSpec((QUARTER, width), column),
-            pl.BlockSpec(rows.shape, lambda i: (0, 0)),
-            pl.BlockSpec((weight.shape[0], width), column),
-        ],
-        out_specs=pl.BlockSpec((QUARTER, width), column),
+        in_specs=[vmem] * 3,
+        out_specs=vmem,
         out_shape=jax.ShapeDtypeStruct(total.shape, BF16),
         compiler_params=pltpu.CompilerParams(vmem_limit_bytes=LESS_VMEM_BYTES),
         cost_estimate=SMALL,

time: 91.2 us -> 89.5 us (0.981)
  Pallas kernels: 33.9 us -> 32.2 us
  transfers between devices with their start and end apart: 13 -> 13, of which waited for: 4 -> 4; matrix products, arithmetic and copies ran while one was open for 0% -> 0% of each run, Pallas kernels for 30% -> 29%
where the time goes in v4:
time: 89.5 us; the launch traced here: 89.1 us
  starting transfers between devices  39.6 us (44%)
  Pallas kernels  32.2 us (36%)
  waiting for transfers between devices  17.1 us (19%)
    ppermute x9, starting transfers between devices, swap(): lax.ppermute(shard, axis, [(i, i ^ bits) for i in range(lax.axis_size(axi...  14.5 us
    all_to_all x1, waiting for transfers between devices, local(): lax.all_to_all(back, ('ctx', 'tp'), 0, 0, axis_index_groups=owners, tiled...  13.8 us
    pallas_call x1, Pallas kernels, local_attention(): pl.pallas_call(local_kernel, grid=(queries.shape[1] // PAIR,), in_specs=[...  13.7 us
    all_to_all x1, starting transfers between devices, local(): lax.all_to_all(back, ('ctx', 'tp'), 0, 0, axis_index_groups=owners, tiled...  9.35 us
    all_to_all x1, starting transfers between devices, local(): lax.all_to_all(picked, 'ctx', 0, 0, axis_index_groups=segments, tiled=True)  9.08 us
    pallas_call x1, Pallas kernels, finish(): pl.pallas_call(finish_kernel, in_specs=[pl.BlockSpec(memory_space=pltpu.S...  6.26 us
    pallas_call x1, Pallas kernels, pick(): pl.pallas_call(pick_kernel, grid=(heads // 2,), in_specs=[pl.BlockSpec(me...  4.32 us
    all_to_all x1, starting transfers between devices, local(): pack = lax.all_to_all(pack, 'tp', 0, 0, tiled=True)  3.91 us
  transfers between devices with their start and end apart: 13, of which 4 were waited for; matrix products, arithmetic and copies ran while one was open for 0% of the time, Pallas kernels for 29%

profile of v4, /device:TPU:1, one launch (start us, length us, event | category | flops | bytes accessed | tf_op | source)
XLA Modules:
  0.0 89.1 jit_solution(9308821659685594153)
XLA Ops:
  0.0 4.3 %pick_rows.1 = bf16[8,288,128]{2,1,0:T(8,128)(2,1)} custom-call(s32[2,32]{1,0:T(2,128)} %bitcast.10, bf16[1024,512]{1,0:T(8,128)(2,1)} %q_ref.3, bf16[1024,512]{1,0:T(8,128)(2,1)} %k_ref.3, bf16[1024,512]{1,0:T(8,128)(2,1)} %v_ref.3), custom_call_target="tpu_custom_call" | custom-call | flops 1000 | bytes 1000 | tf_op jit(solution)/shard_map/pick_rows/pallas_call | solution.py:97
  4.3 9.1 %all-to-all-start = ((bf16[8,288,128]{2,1,0:T(8,128)(2,1)}), bf16[8,288,128]{2,1,0:T(8,128)(2,1)S(1)}, u32[]{:S(2)}, u32[]{:S(2)}) async-start(bf16[8,288,128]{2,1,0:T(8,128)(2,1)} %pick_rows.1), calls=%async_computation | async-start | bytes 1179648 | tf_op jit(solution)/shard_map/all_to_all | solution.py:415
  13.4 2.8 %collective-permute-start.7 = (bf16[512,2048]{1,0:T(8,128)(2,1)}, bf16[512,2048]{1,0:T(8,128)(2,1)}, u32[]{:S(2)}, u32[]{:S(2)}) collective-permute-start(bf16[512,2048]{1,0:T(8,128)(2,1)} %refs_0_.1), channel_id=1, source_target_pairs={{0,2},{1,7},{2,0},{3,5},{4,6},{5,3},{6,4},{7,1},{8,10},{9,15},{10,... | collective-permute-start | bytes 6291464 | tf_op jit(solution)/shard_map/ppermute | solution.py:416
  16.2 13.7 %local_attention.1 = bf16[1024,640]{1,0:T(8,128)(2,1)} custom-call(bf16[1024,512]{1,0:T(8,128)(2,1)} %q_ref.3, bf16[1024,512]{1,0:T(8,128)(2,1)} %k_ref.3, bf16[1024,512]{1,0:T(8,128)(2,1)} %v_ref.3), custom_call_target="tpu_custom_call" | custom-call | flops 1000 | bytes 1000 | tf_op jit(solution)/shard_map/local_attention/pallas_call | solution.py:158
  29.8 0.0 all-to-all-done.sent_ref
  29.8 3.9 %all-to-all-start.1 = ((bf16[4,256,640]{2,1,0:T(8,128)(2,1)}), bf16[4,256,640]{2,1,0:T(8,128)(2,1)S(1)}, u32[]{:S(2)}, u32[]{:S(2)}) async-start(bf16[4,256,640]{2,1,0:T(8,128)(2,1)} %bitcast.12), calls=%async_computation.1 | async-start | bytes 2621440 | tf_op jit(solution)/shard_map/all_to_all | solution.py:423
  33.8 4.3 %collective-permute-start.3 = (bf16[512,128]{1,0:T(8,128)(2,1)S(1)}, bf16[512,128]{1,0:T(8,128)(2,1)S(1)}, u32[]{:S(2)}, u32[]{:S(2)}) collective-permute-start(bf16[512,128]{1,0:T(8,128)(2,1)S(1)} %bitcast.5), channel_id=1, source_target_pairs={{0,32},{4,36},{8,40},{12,44},{16,48},{20,52},{24,56},{28,60},{32,0... | collective-permute-start | bytes 393224 | tf_op jit(solution)/shard_map/ppermute | solution.py:403
  38.1 2.5 %collective-permute-start.2 = (bf16[512,128]{1,0:T(8,128)(2,1)S(1)}, bf16[512,128]{1,0:T(8,128)(2,1)S(1)}, u32[]{:S(2)}, u32[]{:S(2)}) collective-permute-start(bf16[512,128]{1,0:T(8,128)(2,1)S(1)} %bitcast.6), channel_id=1, source_target_pairs={{0,192},{4,196},{8,200},{12,204},{16,208},{20,212},{24,216},{28,22... | collective-permute-start | bytes 393224 | tf_op jit(solution)/shard_map/ppermute | solution.py:403
  40.5 0.5 collective-permute-start.1
  41.1 0.3 collective-permute-start
  41.3 1.5 %collective-permute-done.3.far0_ref = bf16[512,128]{1,0:T(8,128)(2,1)S(1)} collective-permute-done((bf16[512,128]{1,0:T(8,128)(2,1)S(1)}, bf16[512,128]{1,0:T(8,128)(2,1)S(1)}, u32[]{:S(2)}, u32[]{:S(2)}) %collective-permute-start.3) | collective-permute-done | bytes 131104 | tf_op jit(solution)/shard_map/ppermute | solution.py:403
  42.8 2.5 %collective-permute-start.6 = (bf16[512,128]{1,0:T(8,128)(2,1)S(1)}, bf16[512,128]{1,0:T(8,128)(2,1)S(1)}, u32[]{:S(2)}, u32[]{:S(2)}) collective-permute-start(bf16[512,128]{1,0:T(8,128)(2,1)S(1)} %collective-permute-done.3.far0_ref), channel_id=1, source_target_pairs={{0,192},{4,196},{8,200},{12,204},{16,208},{20,212},{24,216},{28,22... | collective-permute-start | bytes 393224 | tf_op jit(solution)/shard_map/ppermute | solution.py:403
  45.3 0.6 collective-permute-done.2.far3_ref
  46.0 1.7 %collective-permute-start.5 = (bf16[512,128]{1,0:T(8,128)(2,1)S(1)}, bf16[512,128]{1,0:T(8,128)(2,1)S(1)}, u32[]{:S(2)}, u32[]{:S(2)}) collective-permute-start(bf16[512,128]{1,0:T(8,128)(2,1)S(1)} %collective-permute-done.3.far0_ref), channel_id=1, source_target_pairs={{0,128},{4,132},{8,136},{12,140},{16,144},{20,148},{24,152},{28,15... | collective-permute-start | bytes 393224 | tf_op jit(solution)/shard_map/ppermute | solution.py:403
  47.7 0.0 collective-permute-done.1.far2_ref
  47.7 2.4 %collective-permute-start.4 = (bf16[512,128]{1,0:T(8,128)(2,1)S(1)}, bf16[512,128]{1,0:T(8,128)(2,1)S(1)}, u32[]{:S(2)}, u32[]{:S(2)}) collective-permute-start(bf16[512,128]{1,0:T(8,128)(2,1)S(1)} %collective-permute-done.3.far0_ref), channel_id=1, source_target_pairs={{0,64},{4,68},{8,72},{12,76},{16,80},{20,84},{24,88},{28,92},{32,9... | collective-permute-start | bytes 393224 | tf_op jit(solution)/shard_map/ppermute | solution.py:403
  50.1 1.9 %near_attention.1.near_ref = bf16[32,32,128]{2,1,0:T(8,128)(2,1)S(1)} custom-call(bf16[8,288,128]{2,1,0:T(8,128)(2,1)S(1)} %all-to-all-done.sent_ref), custom_call_target="tpu_custom_call" | custom-call | flops 1000 | bytes 1000 | tf_op jit(solution)/shard_map/near_attention/pallas_call | solution.py:240
  52.0 0.0 copy-start
  52.0 0.0 collective-permute-done.far1_ref
  52.0 1.8 %first_far_attention.1 = (f32[512,128]{1,0:T(8,128)S(1)}, f32[512,128]{1,0:T(8,128)S(1)}) custom-call(bf16[8,288,128]{2,1,0:T(8,128)(2,1)S(1)} %all-to-all-done.sent_ref, bf16[512,128]{1,0:T(8,128)(2,1)S(1)} %bitcast.9, bf16[512,128]{1,0:T(8,128)(2,1)S(1)} %collective-permute-done.far1_ref, bf16[512,128]{1,0:T(8,128)(2,1)S(1)} %collective-permute-done.1.far2_ref, ...), custom_call_target="tpu_custom_call" | custom-call | flops 1000 | bytes 1000 | tf_op jit(solution)/shard_map/first_far_attention/pallas_call | solution.py:252
  53.8 0.0 collective-permute-done.6.far3_ref
  53.8 0.0 collective-permute-done.5.far2_ref
  53.8 1.1 %collective-permute-done.4.far1_ref = bf16[512,128]{1,0:T(8,128)(2,1)S(1)} collective-permute-done((bf16[512,128]{1,0:T(8,128)(2,1)S(1)}, bf16[512,128]{1,0:T(8,128)(2,1)S(1)}, u32[]{:S(2)}, u32[]{:S(2)}) %collective-permute-start.4) | collective-permute-done | bytes 131104 | tf_op jit(solution)/shard_map/ppermute | solution.py:403
  54.9 2.6 %second_far_attention.1 = bf16[32,48,128]{2,1,0:T(8,128)(2,1)} custom-call(bf16[8,288,128]{2,1,0:T(8,128)(2,1)S(1)} %all-to-all-done.sent_ref, bf16[32,32,128]{2,1,0:T(8,128)(2,1)S(1)} %near_attention.1.near_ref, f32[512,128]{1,0:T(8,128)S(1)} %get-tuple-element.38.held_ref, f32[512,128]{1,0:T(8,128)S(1)} %get-tuple-element.39.held_lse_ref, ...), custom_call_target="tpu_custom_call" | custom-call | flops 1000 | bytes 1000 | tf_op jit(solution)/shard_map/second_far_attention/pallas_call | solution.py:264
  57.6 0.0 all-to-all-done.1
  57.6 9.3 %all-to-all-start.2 = ((bf16[32,48,128]{2,1,0:T(8,128)(2,1)}), bf16[32,48,128]{2,1,0:T(8,128)(2,1)S(1)}, u32[]{:S(2)}, u32[]{:S(2)}) async-start(bf16[32,48,128]{2,1,0:T(8,128)(2,1)} %second_far_attention.1), calls=%async_computation.2 | async-start | bytes 786432 | tf_op jit(solution)/shard_map/all_to_all | solution.py:433
  66.9 0.3 collective-permute-start.8
  67.2 0.0 collective-permute-done.7.refs_2_
  67.3 13.8 %all-to-all-done.2.back_ref = bf16[32,48,128]{2,1,0:T(8,128)(2,1)S(1)} async-done(((bf16[32,48,128]{2,1,0:T(8,128)(2,1)}), bf16[32,48,128]{2,1,0:T(8,128)(2,1)S(1)}, u32[]{:S(2)}, u32[]{:S(2)}) %all-to-all-start.2) | async-done | bytes 393248 | tf_op jit(solution)/shard_map/all_to_all | solution.py:433
  81.1 0.0 collective-permute-start.9
  81.1 0.0 collective-permute-done.8.refs_1_
  81.1 0.0 copy-done
  81.1 6.3 %finish.1 = (f32[256,2048]{1,0:T(8,128)S(1)}, bf16[256,512]{1,0:T(8,128)(2,1)S(1)}) custom-call(s32[2,32]{1,0:T(2,128)S(1)} %bitcast.11, bf16[1024,640]{1,0:T(8,128)(2,1)S(1)} %bitcast.4, bf16[32,48,128]{2,1,0:T(8,128)(2,1)S(1)} %all-to-all-done.2.back_ref, bf16[512,2048]{1,0:T(8,128)(2,1)} %refs_0_.1, bf16[512,2048]{1,0:T(8,128)(2,1)} %collective-permute-done.8.refs_1_, ...), custom_call_target="tpu_custom_call" | custom-call | flops 1000 | bytes 1000 | tf_op jit(solution)/shard_map/finish/pallas_call | solution.py:362
  87.4 0.0 collective-permute-done.9.weight_ref
  87.4 1.7 %add_last.1 = bf16[256,2048]{1,0:T(8,128)(2,1)} custom-call(f32[256,2048]{1,0:T(8,128)S(1)} %get-tuple-element.51.total_ref, bf16[256,512]{1,0:T(8,128)(2,1)S(1)} %get-tuple-element.52.rows_ref, bf16[512,2048]{1,0:T(8,128)(2,1)S(1)} %collective-permute-done.9.weight_ref), custom_call_target="tpu_custom_call" | custom-call | flops 1000 | bytes 1000 | tf_op jit(solution)/shard_map/add_last/pallas_call | solution.py:391
  (1 shorter events, 0.0 us)
Async XLA Ops:
  4.3 25.5 %all-to-all-start = ((bf16[8,288,128]{2,1,0:T(8,128)(2,1)}), bf16[8,288,128]{2,1,0:T(8,128)(2,1)S(1)}, u32[]{:S(2)}, u32[]{:S(2)}) async-start(bf16[8,288,128]{2,1,0:T(8,128)(2,1)} %pick_rows.1), calls=%async_computation | async-start | bytes 1179648 | tf_op jit(solution)/shard_map/all_to_all | solution.py:415
  13.4 53.8 %collective-permute-start.7 = (bf16[512,2048]{1,0:T(8,128)(2,1)}, bf16[512,2048]{1,0:T(8,128)(2,1)}, u32[]{:S(2)}, u32[]{:S(2)}) collective-permute-start(bf16[512,2048]{1,0:T(8,128)(2,1)} %refs_0_.1), channel_id=1, source_target_pairs={{0,2},{1,7},{2,0},{3,5},{4,6},{5,3},{6,4},{7,1},{8,10},{9,15},{10,... | collective-permute-start | bytes 6291464 | tf_op jit(solution)/shard_map/ppermute | solution.py:416
  29.8 27.7 %all-to-all-start.1 = ((bf16[4,256,640]{2,1,0:T(8,128)(2,1)}), bf16[4,256,640]{2,1,0:T(8,128)(2,1)S(1)}, u32[]{:S(2)}, u32[]{:S(2)}) async-start(bf16[4,256,640]{2,1,0:T(8,128)(2,1)} %bitcast.12), calls=%async_computation.1 | async-start | bytes 2621440 | tf_op jit(solution)/shard_map/all_to_all | solution.py:423
  33.8 9.1 %collective-permute-start.3 = (bf16[512,128]{1,0:T(8,128)(2,1)S(1)}, bf16[512,128]{1,0:T(8,128)(2,1)S(1)}, u32[]{:S(2)}, u32[]{:S(2)}) collective-permute-start(bf16[512,128]{1,0:T(8,128)(2,1)S(1)} %bitcast.5), channel_id=1, source_target_pairs={{0,32},{4,36},{8,40},{12,44},{16,48},{20,52},{24,56},{28,60},{32,0... | collective-permute-start | bytes 393224 | tf_op jit(solution)/shard_map/ppermute | solution.py:403
  38.1 7.9 %collective-permute-start.2 = (bf16[512,128]{1,0:T(8,128)(2,1)S(1)}, bf16[512,128]{1,0:T(8,128)(2,1)S(1)}, u32[]{:S(2)}, u32[]{:S(2)}) collective-permute-start(bf16[512,128]{1,0:T(8,128)(2,1)S(1)} %bitcast.6), channel_id=1, source_target_pairs={{0,192},{4,196},{8,200},{12,204},{16,208},{20,212},{24,216},{28,22... | collective-permute-start | bytes 393224 | tf_op jit(solution)/shard_map/ppermute | solution.py:403
  40.5 7.2 %collective-permute-start.1 = (bf16[512,128]{1,0:T(8,128)(2,1)S(1)}, bf16[512,128]{1,0:T(8,128)(2,1)S(1)}, u32[]{:S(2)}, u32[]{:S(2)}) collective-permute-start(bf16[512,128]{1,0:T(8,128)(2,1)S(1)} %bitcast.7), channel_id=1, source_target_pairs={{0,128},{4,132},{8,136},{12,140},{16,144},{20,148},{24,152},{28,15... | collective-permute-start | bytes 393224 | tf_op jit(solution)/shard_map/ppermute | solution.py:403
  41.1 10.9 %collective-permute-start = (bf16[512,128]{1,0:T(8,128)(2,1)S(1)}, bf16[512,128]{1,0:T(8,128)(2,1)S(1)}, u32[]{:S(2)}, u32[]{:S(2)}) collective-permute-start(bf16[512,128]{1,0:T(8,128)(2,1)S(1)} %bitcast.8), channel_id=1, source_target_pairs={{0,64},{4,68},{8,72},{12,76},{16,80},{20,84},{24,88},{28,92},{32,9... | collective-permute-start | bytes 393224 | tf_op jit(solution)/shard_map/ppermute | solution.py:403
  42.8 10.9 %collective-permute-start.6 = (bf16[512,128]{1,0:T(8,128)(2,1)S(1)}, bf16[512,128]{1,0:T(8,128)(2,1)S(1)}, u32[]{:S(2)}, u32[]{:S(2)}) collective-permute-start(bf16[512,128]{1,0:T(8,128)(2,1)S(1)} %collective-permute-done.3.far0_ref), channel_id=1, source_target_pairs={{0,192},{4,196},{8,200},{12,204},{16,208},{20,212},{24,216},{28,22... | collective-permute-start | bytes 393224 | tf_op jit(solution)/shard_map/ppermute | solution.py:403
  46.0 7.8 %collective-permute-start.5 = (bf16[512,128]{1,0:T(8,128)(2,1)S(1)}, bf16[512,128]{1,0:T(8,128)(2,1)S(1)}, u32[]{:S(2)}, u32[]{:S(2)}) collective-permute-start(bf16[512,128]{1,0:T(8,128)(2,1)S(1)} %collective-permute-done.3.far0_ref), channel_id=1, source_target_pairs={{0,128},{4,132},{8,136},{12,140},{16,144},{20,148},{24,152},{28,15... | collective-permute-start | bytes 393224 | tf_op jit(solution)/shard_map/ppermute | solution.py:403
  47.7 7.2 %collective-permute-start.4 = (bf16[512,128]{1,0:T(8,128)(2,1)S(1)}, bf16[512,128]{1,0:T(8,128)(2,1)S(1)}, u32[]{:S(2)}, u32[]{:S(2)}) collective-permute-start(bf16[512,128]{1,0:T(8,128)(2,1)S(1)} %collective-permute-done.3.far0_ref), channel_id=1, source_target_pairs={{0,64},{4,68},{8,72},{12,76},{16,80},{20,84},{24,88},{28,92},{32,9... | collective-permute-start | bytes 393224 | tf_op jit(solution)/shard_map/ppermute | solution.py:403
  52.0 29.1 %copy-start = (s32[32,2]{0,1:T(2,128)S(1)}, s32[32,2]{0,1:T(2,128)}, u32[]{:S(2)}) copy-start(s32[32,2]{0,1:T(2,128)} %param.8) | copy-start | bytes 772
  57.6 23.5 %all-to-all-start.2 = ((bf16[32,48,128]{2,1,0:T(8,128)(2,1)}), bf16[32,48,128]{2,1,0:T(8,128)(2,1)S(1)}, u32[]{:S(2)}, u32[]{:S(2)}) async-start(bf16[32,48,128]{2,1,0:T(8,128)(2,1)} %second_far_attention.1), calls=%async_computation.2 | async-start | bytes 786432 | tf_op jit(solution)/shard_map/all_to_all | solution.py:433
  66.9 14.2 %collective-permute-start.8 = (bf16[512,2048]{1,0:T(8,128)(2,1)}, bf16[512,2048]{1,0:T(8,128)(2,1)}, u32[]{:S(2)}, u32[]{:S(2)}) collective-permute-start(bf16[512,2048]{1,0:T(8,128)(2,1)} %refs_0_.1), channel_id=1, source_target_pairs={{0,1},{1,0},{2,3},{3,2},{4,5},{5,4},{6,7},{7,6},{8,9},{9,8},{10,11... | collective-permute-start | bytes 6291464 | tf_op jit(solution)/shard_map/ppermute | solution.py:403
  81.1 6.3 %collective-permute-start.9 = (bf16[512,2048]{1,0:T(8,128)(2,1)}, bf16[512,2048]{1,0:T(8,128)(2,1)S(1)}, u32[]{:S(2)}, u32[]{:S(2)}) collective-permute-start(bf16[512,2048]{1,0:T(8,128)(2,1)} %collective-permute-done.7.refs_2_), channel_id=1, source_target_pairs={{0,1},{1,0},{2,3},{3,2},{4,5},{5,4},{6,7},{7,6},{8,9},{9,8},{10,11... | collective-permute-start | bytes 6291464 | tf_op jit(solution)/shard_map/ppermute | solution.py:403
